TPU v7x, 32 devices: a whole 2x2x4 slice. The times are simulated.
32 devices in a mesh: wave: 16 (over z, y, core), lev: 2 (over x).
Axes of the slice: x: 2, y: 2, z: 4, core: 2. Of those that a mesh axis runs over, the one named last changes fastest.
Arguments:
- spectral: bfloat16 [6, 2, 2, 640, 640], P('lev', None, None, 'wave'), may hold values from -0.0059814453 to 0.0059814453
- legendre: bfloat16 [640, 1280, 640], P('wave', 'lev'), may hold values from -6 to 6
- thickness: float32 [6], replicated, may hold values from 0.03 to 0.3
- pressure_step: float32 [6], replicated, may hold values from 0.03 to 0.3
- wave_order: int32 [640], replicated, may hold values from 0 to 639, as said below
- lat_order: int32 [1280], replicated, may hold values from 0 to 1279, each once
Outputs:
- spectral_out: float32 [6, 2, 2, 640, 640], P('lev', None, None, 'wave')
Inputs may be any that keep to these rules, and one draw needn't show every extreme that they name: `wave_order`: slots 2 p and 2 p + 1 hold the wavenumbers w and 639 - w for some w < 320, the smaller first; every wavenumber appears once. `lat_order`: every latitude index appears once.
All inputs are finite; a program needn't handle non-finite values.
Results may differ from a plain program's by a relative error of at most 0.0046.
Values may be sent and summed in bfloat16 or wider, within the bound.
A program may use at most 128 MiB of HBM per device.

v0:
```python
import math

import jax
import jax.numpy as jnp
from jax import lax
from jax.sharding import PartitionSpec as P

M = 640
NLAT = 1280
NLON = 2560


def wave_tables(wave_list, lon_total):
    lon_ids = jnp.arange(lon_total, dtype=jnp.int32)
    phases = wave_list[:, None] * lon_ids[None, :] % lon_total
    angles = phases.astype(jnp.float32) * (2.0 * math.pi / lon_total)
    cosine = jnp.cos(angles)
    sine_part = jnp.sin(angles)
    weights = jnp.where(wave_list == 0, 1.0, 2.0).astype(jnp.float32)[:, None]
    inverse = jnp.stack([weights * cosine, -(weights * sine_part)], axis=0).astype(jnp.bfloat16)
    factor = 2.0 / lon_total
    direct = jnp.stack([factor * cosine, -(factor * sine_part)], axis=0)
    direct = jnp.transpose(direct, (2, 0, 1)).astype(jnp.bfloat16)
    return (inverse, direct)


def mix_levels(temper, diverg, geopot, omega_vel, sin_lat):
    first_field = geopot + omega_vel * temper
    second_field = sin_lat[None, :, None] * omega_vel + diverg * temper
    return jnp.stack([first_field, second_field], axis=1).astype(jnp.bfloat16)


def body(spectral, legendre, thickness, pressure_step, wave_order, lat_order):
    wave_index = lax.axis_index("wave")
    wave_count = lax.axis_size("wave")
    local_slots = legendre.shape[0]
    grid_lats = NLAT // wave_count
    my_waves = lax.dynamic_slice(wave_order, (wave_index * local_slots,), (local_slots,))
    row_ids = jnp.arange(M, dtype=jnp.int32)
    in_triangle = row_ids[None, :] < (M - my_waves)[:, None]
    masked_leg = jnp.where(in_triangle[:, None, :], legendre, jnp.zeros((), jnp.bfloat16))
    fourier = jnp.einsum(
        "lfcsk,sqk->lfcsq",
        lax.all_gather(spectral, "lev", axis=0, tiled=True),
        masked_leg,
        preferred_element_type=jnp.float32,
    ).astype(jnp.bfloat16)
    level_split = lax.all_to_all(fourier, "lev", split_axis=0, concat_axis=4, tiled=True)
    inverse_table, forward_legendre_table = wave_tables(wave_order, NLON)
    grid_vals = jnp.einsum(
        "lfcsq,cst->lfqt",
        lax.all_to_all(level_split, "wave", split_axis=4, concat_axis=3, tiled=True),
        inverse_table,
        preferred_element_type=jnp.float32,
    )
    lat_ids = lax.dynamic_slice(lat_order, (wave_index * grid_lats,), (grid_lats,))
    angles = math.pi * (lat_ids.astype(jnp.float32) + 0.75) / (NLAT + 0.5)
    sin_lat = jnp.cos(angles)
    cos_lat = jnp.sin(angles)
    columns = lax.all_to_all(grid_vals, "lev", split_axis=3, concat_axis=0, tiled=True)
    temper = columns[:, 0]
    diverg = columns[:, 1]
    geopot = jnp.flip(jnp.cumsum(jnp.flip(thickness[:, None, None] * temper, 0), axis=0), 0)
    omega_vel = -jnp.cumsum(pressure_step[:, None, None] * diverg, axis=0)
    tend_cols = mix_levels(temper, diverg, geopot, omega_vel, sin_lat)
    tendency_field = lax.all_to_all(tend_cols, "lev", split_axis=0, concat_axis=3, tiled=True)
    returned_grid_values = (
        jnp.einsum(
            "opgu,ukh->opkhg",
            tendency_field,
            forward_legendre_table,
            preferred_element_type=jnp.float32,
        )
        * cos_lat
    ).astype(jnp.bfloat16)
    band_vals = lax.all_to_all(
        lax.all_to_all(returned_grid_values, "wave", split_axis=3, concat_axis=4, tiled=True),
        "lev",
        split_axis=4,
        concat_axis=0,
        tiled=True,
    )
    summed = lax.psum_scatter(
        jnp.einsum("lfcsq,sqk->lfcsk", band_vals, masked_leg, preferred_element_type=jnp.float32),
        "lev",
        scatter_dimension=0,
        tiled=True,
    )
    return summed


def solution(mesh):
    in_specs = (P("lev", None, None, "wave", None), P("wave", "lev", None), P(), P(), P(), P())
    out_specs = P("lev", None, None, "wave", None)
    return jax.shard_map(body, mesh=mesh, in_specs=in_specs, out_specs=out_specs, check_vma=False)
```

profile of v0, /device:TPU:0, one launch (start us, length us, event | category | flops | bytes accessed | tf_op | source)
XLA Modules:
  0.0 486.1 jit_solution(3468522964204752684)
XLA Ops:
  6.5 0.0 all-gather.2.cloned.1.call-start
  6.5 0.7 all-gather.2.cloned.1.call-update
  7.3 0.8 dynamic-slice_subtract_fusion
  8.0 0.1 iota_compare_fusion
  8.1 26.8 %all-gather.2.cloned.1.call-done = bf16[6,2,2,40,640]{4,3,2,1,0:T(8,128)(2,1)} async-done(((bf16[3,2,2,40,640]{4,3,2,1,0:T(8,128)(2,1)}), bf16[6,2,2,40,640]{4,3,2,1,0:T(8,128)(2,1)}) %all-gather.2.cloned.1.call-update) | async-done | bytes 1228816 | tf_op jit(solution)/shard_map/all_gather | solution.py:44
  35.0 16.7 %fusion.33 = bf16[6,2,2,40,640]{4,0,2,1,3:T(8,128)(2,1)S(1)} fusion(bf16[6,2,2,40,640]{4,3,2,1,0:T(8,128)(2,1)} %all-gather.2.cloned.1.call-done, bf16[40,640,640]{2,1,0:T(8,128)(2,1)} %param.7, pred[40,640]{1,0:T(8,128)(4,1)S(1)} %iota_compare_fusion), kind=kOutput, calls=%fused_computation.46 | convolution fusion | flops 803430400 | bytes 35251200 | tf_op jit(solution)/shard_map/lfcsk,sqk->lfcsq/dot_general | solution.py:42
  51.7 0.4 copy.48
  52.1 18.3 %all_to_all.108 = bf16[6,2,2,40,640]{4,3,2,1,0:T(8,128)(2,1)S(1)} all-to-all(bf16[6,2,2,40,640]{4,3,2,1,0:T(8,128)(2,1)S(1)} %copy.48), channel_id=1, replica_groups=mesh['wave'=16,'lev'=2] {'lev'}, dimensions={0} | all-to-all | bytes 2457600 | tf_op jit(solution)/shard_map/all_to_all | solution.py:48
  70.4 6.2 %copy.77 = bf16[3,2,2,40,2,640]{3,2,1,0,5,4:T(2,128)(2,1)} copy(bf16[3,2,2,40,2,640]{5,3,2,1,0,4:T(8,128)(2,1)S(1)} %bitcast.114) | data formatting | bytes 2457600 | tf_op jit(solution)/shard_map/all_to_all | solution.py:48
  76.6 7.6 %reshape.208 = bf16[16,2,19200]{2,1,0:T(2,128)(2,1)} reshape(bf16[1280,3,2,2,40]{4,3,2,1,0:T(2,128)(2,1)} %bitcast.108) | data formatting | bytes 2457600
  84.2 0.0 copy-start.1
  84.2 5.8 %all-to-all-start.1 = ((bf16[16,2,19200]{2,1,0:T(2,128)(2,1)}), bf16[16,2,19200]{2,1,0:T(2,128)(2,1)S(1)}, u32[]{:S(2)}, u32[]{:S(2)}) async-start(bf16[16,2,19200]{2,1,0:T(2,128)(2,1)} %reshape.208), calls=%async_computation.1 | async-start | bytes 2457600 | tf_op jit(solution)/shard_map/all_to_all | solution.py:52
  90.0 0.0 copy-done.1
  90.0 32.0 %multiply_convert_fusion.1 = (bf16[1,640,2560]{2,1,0:T(8,128)(2,1)}, bf16[1,640,2560]{2,1,0:T(8,128)(2,1)}, bf16[1,640,2560]{2,1,0:T(8,128)(2,1)}, bf16[1,640,2560]{2,1,0:T(8,128)(2,1)}) fusion(s32[640]{0:T(1024)S(1)} %copy-done.1, f32[640]{0:T(1024)S(1)} %compare_select_fusion), kind=kLoop, calls=%fused_computation.21 | loop fusion | flops 31129600 | bytes 13112320 | tf_op jit(solution)/shard_map/convert.5
  122.0 0.0 all-to-all-done.1
  122.0 7.2 %reshape.209 = bf16[1280,3,2,2,40]{4,3,2,1,0:T(2,128)(2,1)} reshape(bf16[16,2,19200]{2,1,0:T(2,128)(2,1)S(1)} %all-to-all-done.1) | data formatting | bytes 2457600
  129.2 0.0 copy-start
  129.2 8.8 %copy.79 = bf16[3,2,2,40,16,80]{5,3,4,2,1,0:T(8,128)(2,1)} copy(bf16[3,2,2,40,16,80]{3,2,1,0,5,4:T(2,128)(2,1)} %bitcast.110) | data formatting | bytes 2457600 | tf_op jit(solution)/shard_map/all_to_all | solution.py:52
  137.9 0.0 copy-done
  137.9 8.1 %fusion.19 = f32[3,2,80,2560]{3,2,1,0:T(8,128)} fusion(bf16[3,2,2,640,80]{4,3,2,1,0:T(8,128)(2,1)} %bitcast.115, bf16[1,640,2560]{2,1,0:T(8,128)(2,1)S(1)} %copy-done, bf16[1,640,2560]{2,1,0:T(8,128)(2,1)} %get-tuple-element.12), kind=kOutput, calls=%fused_computation.28 | convolution fusion | flops 3149004800 | bytes 12697600 | tf_op jit(solution)/shard_map/lfcsq,cst->lfqt/dot_general | solution.py:50
  146.0 10.4 %copy.54 = f32[3,2,80,2560]{2,1,0,3:T(2,128)} copy(f32[3,2,80,2560]{3,2,1,0:T(8,128)} %fusion.19) | data formatting | bytes 9830400 | tf_op jit(solution)/shard_map/lfcsq,cst->lfqt/dot_general | solution.py:50
  156.5 6.8 %all-to-all-start.2 = ((f32[3,2,80,2560]{2,1,0,3:T(2,128)}), f32[3,2,80,2560]{2,1,0,3:T(2,128)}, u32[]{:S(2)}, u32[]{:S(2)}) async-start(f32[3,2,80,2560]{2,1,0,3:T(2,128)} %copy.54), calls=%async_computation.2 | async-start | bytes 15728640 | tf_op jit(solution)/shard_map/all_to_all | solution.py:60
  163.2 0.2 reduce-scatter.2.cloned.1.call-start
  163.5 0.8 fusion.45
  164.3 86.5 %all-to-all-done.2 = f32[3,2,80,2560]{2,1,0,3:T(2,128)} async-done(((f32[3,2,80,2560]{2,1,0,3:T(2,128)}), f32[3,2,80,2560]{2,1,0,3:T(2,128)}, u32[]{:S(2)}, u32[]{:S(2)}) %all-to-all-start.2) | async-done | bytes 4915232 | tf_op jit(solution)/shard_map/all_to_all | solution.py:60
  250.8 10.5 %copy.82 = f32[2,3,2,80,1280]{4,3,1,0,2:T(8,128)} copy(f32[2,3,2,80,1280]{3,2,1,4,0:T(2,128)} %bitcast.19) | data formatting | bytes 9830400 | tf_op jit(solution)/shard_map/all_to_all | solution.py:60
  261.3 0.0 copy-start.2
  261.3 10.4 %copy.56 = f32[2,3,2,80,1280]{4,3,2,1,0:T(8,128)} copy(f32[2,3,2,80,1280]{3,2,1,4,0:T(2,128)} %bitcast.19) | data formatting | bytes 9830400 | tf_op jit(solution)/shard_map/all_to_all | solution.py:60
  271.7 0.0 copy-done.2
  271.7 2.0 bitcast_multiply_fusion.5
  273.7 1.6 rev.7
  275.3 0.0 copy-start.3
  275.3 0.0 slice-start
  275.4 2.0 fusion.47
  277.4 0.0 copy-done.3
  277.4 0.0 slice-start.1
  277.4 3.8 fusion.21
  281.2 0.0 slice-done
  281.2 0.0 slice-done.1
  281.2 0.5 fusion.39
  281.8 0.2 pad_maximum_fusion
  282.0 31.3 %all_to_all.109 = bf16[6,2,80,1280]{3,2,1,0:T(8,128)(2,1)S(1)} all-to-all(bf16[6,2,80,1280]{3,2,1,0:T(8,128)(2,1)S(1)} %pad_maximum_fusion), channel_id=1, replica_groups=mesh['wave'=16,'lev'=2] {'lev'}, dimensions={0} | all-to-all | bytes 4915200 | tf_op jit(solution)/shard_map/all_to_all | solution.py:66
  313.3 2.5 copy.60
  315.9 2.9 reshape.206
  318.7 7.0 %fusion.38 = bf16[3,2,2,640,80]{3,4,1,0,2:T(8,128)(2,1)S(1)} fusion(bf16[3,2,80,2560,1]{3,2,1,0,4:T(8,128)(2,1)} %reshape.206, bf16[1,640,2560]{2,1,0:T(8,128)(2,1)} %get-tuple-element.10, bf16[1,640,2560]{2,1,0:T(8,128)(2,1)} %get-tuple-element.9, f32[80]{0:T(128)S(1)} %get-tuple-element.5), kind=kOutput, calls=%fused_computation.47 | convolution fusion | flops 3160064000 | bytes 10240320 | tf_op jit(solution)/shard_map/opgu,ukh->opkhg/dot_general | solution.py:68
  325.7 2.6 copy.62
  328.3 50.2 %all_to_all.110 = bf16[3,2,2,640,80]{4,1,0,2,3:T(2,128)(2,1)S(1)} all-to-all(bf16[3,2,2,640,80]{4,1,0,2,3:T(2,128)(2,1)S(1)} %copy.62), channel_id=1, replica_groups=mesh['wave'=16,'lev'=2] {'wave'}, dimensions={3} | all-to-all | bytes 2457600 | tf_op jit(solution)/shard_map/all_to_all | solution.py:77
  378.5 0.3 copy.63
  378.9 6.1 %copy.83 = bf16[3,2,2,40,16,80]{3,2,1,0,5,4:T(2,128)(2,1)} copy(bf16[3,2,2,40,16,80]{5,3,4,2,1,0:T(8,128)(2,1)S(1)} %bitcast.113) | data formatting | bytes 2457600 | tf_op jit(solution)/shard_map/all_to_all | solution.py:77
  385.0 7.5 %reshape.210 = bf16[2,2,153600]{2,1,0:T(2,128)(2,1)S(1)} reshape(bf16[1280,3,2,2,40]{4,3,2,1,0:T(2,128)(2,1)} %bitcast.111) | data formatting | bytes 2457600
  392.5 19.2 %all_to_all.111 = bf16[2,2,153600]{2,1,0:T(2,128)(2,1)S(1)} all-to-all(bf16[2,2,153600]{2,1,0:T(2,128)(2,1)S(1)} %reshape.210), channel_id=1, replica_groups=mesh['wave'=16,'lev'=2] {'lev'}, dimensions={0} | all-to-all | bytes 2457600 | tf_op jit(solution)/shard_map/all_to_all | solution.py:76
  411.7 7.5 %reshape.211 = bf16[1280,3,2,2,40]{4,3,2,1,0:T(2,128)(2,1)} reshape(bf16[2,2,153600]{2,1,0:T(2,128)(2,1)S(1)} %all_to_all.111) | data formatting | bytes 2457600
  419.2 8.5 %copy.67 = bf16[2,3,2,2,40,640]{5,4,3,2,1,0:T(8,128)(2,1)} copy(bf16[2,3,2,2,40,640]{4,3,2,1,5,0:T(2,128)(2,1)} %bitcast.109) | data formatting | bytes 2457600 | tf_op jit(solution)/shard_map/all_to_all | solution.py:76
  427.7 14.2 %fusion.25 = f32[6,2,2,40,640]{4,0,2,1,3:T(8,128)S(1)} fusion(bf16[40,640,640]{2,1,0:T(8,128)(2,1)} %param.7, pred[40,640]{1,0:T(8,128)(4,1)S(1)} %iota_compare_fusion, bf16[6,2,2,40,640]{4,3,2,1,0:T(8,128)(2,1)} %bitcast.116), kind=kOutput, calls=%fused_computation.42 | convolution fusion | flops 802816000 | bytes 36480000 | tf_op jit(solution)/shard_map/lfcsq,sqk->lfcsk/dot_general | solution.py:84
  441.9 2.9 copy.69
  444.8 0.0 reduce-scatter.2.cloned.1.call-update
  444.8 34.4 %reduce-scatter.2.cloned.1.call-done = f32[3,2,2,40,640]{4,3,2,1,0:T(8,128)} async-done(((f32[6,2,2,40,640]{4,3,2,1,0:T(8,128)}), f32[3,2,2,40,640]{4,3,2,1,0:T(8,128)}) %reduce-scatter.2.cloned.1.call-update) | async-done | bytes 1228816 | tf_op jit(solution)/shard_map/reduce_scatter | solution.py:83
  (2 shorter events, 0.0 us)
Async XLA Ops:
  6.5 28.4 %all-gather.2.cloned.1.call-start = ((), (), s32[]{:S(2)}) async-start(), calls=%async_computation.7 | async-start | bytes 1843200 | tf_op jit(solution)/shard_map/all_gather | solution.py:44
  84.2 5.8 %copy-start.1 = (s32[640]{0:T(1024)S(1)}, s32[640]{0:T(1024)}, u32[]{:S(2)}) copy-start(s32[640]{0:T(1024)} %param.10) | copy-start | bytes 7684
  84.2 37.8 %all-to-all-start.1 = ((bf16[16,2,19200]{2,1,0:T(2,128)(2,1)}), bf16[16,2,19200]{2,1,0:T(2,128)(2,1)S(1)}, u32[]{:S(2)}, u32[]{:S(2)}) async-start(bf16[16,2,19200]{2,1,0:T(2,128)(2,1)} %reshape.208), calls=%async_computation.1 | async-start | bytes 2457600 | tf_op jit(solution)/shard_map/all_to_all | solution.py:52
  129.2 8.8 %copy-start = (bf16[1,640,2560]{2,1,0:T(8,128)(2,1)S(1)}, bf16[1,640,2560]{2,1,0:T(8,128)(2,1)}, u32[]{:S(2)}) copy-start(bf16[1,640,2560]{2,1,0:T(8,128)(2,1)} %get-tuple-element.11) | copy-start | bytes 9830404
  156.5 94.4 %all-to-all-start.2 = ((f32[3,2,80,2560]{2,1,0,3:T(2,128)}), f32[3,2,80,2560]{2,1,0,3:T(2,128)}, u32[]{:S(2)}, u32[]{:S(2)}) async-start(f32[3,2,80,2560]{2,1,0,3:T(2,128)} %copy.54), calls=%async_computation.2 | async-start | bytes 15728640 | tf_op jit(solution)/shard_map/all_to_all | solution.py:60
  163.2 316.0 %reduce-scatter.2.cloned.1.call-start = ((), (), s32[]{:S(2)}) async-start(), calls=%async_computation.8 | async-start | bytes 3686400 | tf_op jit(solution)/shard_map/reduce_scatter | solution.py:83
  261.3 10.4 %copy-start.2 = (f32[6]{0:T(128)S(1)}, f32[6]{0:T(128)}, u32[]{:S(2)}) copy-start(f32[6]{0:T(128)} %param.8) | copy-start | bytes 76
  275.3 2.0 copy-start.3
  275.3 5.9 %slice-start = ((s8[4915200]{0:T(1024)(128)(4,1)}), s8[4194304]{0:T(1024)(128)(4,1)S(1)}, s32[]{:S(2)}) async-start(s8[4915200]{0:T(1024)(128)(4,1)} %bitcast.104), calls=%async_computation.9 | async-start | bytes 8388608
  277.4 3.8 slice-start.1
Sparse Core Ops, SparseCore 0:
  8.9 26.0 all-gather.1
  444.9 34.2 reduce-scatter.1
where the time goes:
time: 488 us; the launch traced here: 486 us
  waiting for transfers between devices  149 us (31%)
  blocking collectives  119 us (24%)
  local copies, waits for them, and re-layouts  104 us (21%)
  matrix products  46 us (9%)
  other arithmetic  42.2 us (9%)
  between operations  13.6 us (3%)
  starting transfers between devices  12.7 us (3%)
    all_to_all x1, waiting for transfers between devices, body(): lax.all_to_all(grid_vals, 'lev', split_axis=3, concat_axis=0, tiled=True)  86.5 us
    all_to_all x1, blocking collectives, body(): lax.all_to_all(returned_grid_values, 'wave', split_axis=3, concat_axis=4,...  50.2 us
    reduce_scatter x1, waiting for transfers between devices, body(): lax.psum_scatter(jnp.einsum('lfcsq,sqk->lfcsk', band_vals, masked_leg, pr...  34.4 us
    another operation x1, other arithmetic  32 us
    all_to_all x1, blocking collectives, body(): lax.all_to_all(tend_cols, 'lev', split_axis=0, concat_axis=3, tiled=True)  31.3 us
    unnamed x16, local copies, waits for them, and re-layouts  29.9 us
    all_gather x1, waiting for transfers between devices, body(): lax.all_gather(spectral, 'lev', axis=0, tiled=True)  26.8 us
    all_to_all x2, local copies, waits for them, and re-layouts, body(): lax.all_to_all(grid_vals, 'lev', split_axis=3, concat_axis=0, tiled=True)  20.9 us
  transfers between devices with their start and end apart: 4, of which 3 were waited for; matrix products, arithmetic and copies ran while one was open for 7% of the time, Pallas kernels for 0%

commit v1 on v0

--- a/solution.py
+++ b/solution.py
@@ -3,6 +3,8 @@
 import jax
 import jax.numpy as jnp
 from jax import lax
+from jax.experimental import pallas as pl
+from jax.experimental.pallas import tpu as pltpu
 from jax.sharding import PartitionSpec as P
 
 M = 640
@@ -30,7 +32,7 @@
     return jnp.stack([first_field, second_field], axis=1).astype(jnp.bfloat16)
 
 
-def body(spectral, legendre, thickness, pressure_step, wave_order, lat_order):
+def general_body(spectral, legendre, thickness, pressure_step, wave_order, lat_order):
     wave_index = lax.axis_index("wave")
     wave_count = lax.axis_size("wave")
     local_slots = legendre.shape[0]
@@ -89,7 +91,260 @@
     return summed
 
 
+LANES = 128
+ROWS = 256
+VMEM_LIMIT = 48 * 1024 * 1024
+
+
+def placed(rows, cols, row_start, col_start, count):
+    r = lax.broadcasted_iota(jnp.int32, (rows, cols), 0)
+    c = lax.broadcasted_iota(jnp.int32, (rows, cols), 1)
+    hit = (r - row_start == c - col_start) & (c >= col_start) & (c < col_start + count)
+    return jnp.where(hit, 1.0, 0.0).astype(jnp.bfloat16)
+
+
+def inverse_legendre_kernel(slots, lats, lv, nw, spec_ref, leg_ref, out_ref, cut, held):
+    s = pl.program_id(0)
+    tiles = cut.shape[0]
+
+    @pl.when(s == 0)
+    def _():
+        for b in range(tiles):
+            cut[b] = spec_ref[:, b * LANES : (b + 1) * LANES]
+
+    x = jnp.concatenate([cut[b, pl.ds(s, 8 * lv, stride=slots), :] for b in range(tiles)], axis=1).astype(jnp.bfloat16)
+    y = lax.dot_general(x, leg_ref[0], (((1,), (1,)), ((), ())), preferred_element_type=jnp.float32)
+    blocks = y.shape[1] // LANES
+    for l in range(lv):
+        for b in range(blocks):
+            held[l * blocks + b, pl.ds(s, 8, stride=slots), :] = y[8 * l : 8 * l + 8, b * LANES : (b + 1) * LANES]
+
+    @pl.when(s == slots - 1)
+    def _():
+        for d in range(nw):
+            total = jnp.zeros((8 * slots, LANES), jnp.float32)
+            for b in range(lats * d // LANES, (lats * (d + 1) - 1) // LANES + 1):
+                for l in range(lv):
+                    first = max(lats * d, LANES * b)
+                    last = min(lats * (d + 1), LANES * (b + 1))
+                    sel = placed(LANES, LANES, first - LANES * b, lats * l + first - lats * d, last - first)
+                    total += jnp.dot(held[l * blocks + b].astype(jnp.bfloat16), sel, preferred_element_type=jnp.float32)
+            out_ref[d] = total.astype(jnp.bfloat16)
+
+
+def inverse_legendre(spec, legendre, lv, nw):
+    slots, band, rows = legendre.shape
+    lats = band // nw
+    return pl.pallas_call(
+        lambda *refs: inverse_legendre_kernel(slots, lats, lv, nw, *refs),
+        grid=(slots,),
+        in_specs=[
+            pl.BlockSpec((8 * lv * slots, rows), lambda s: (0, 0)),
+            pl.BlockSpec((1, band, rows), lambda s: (s, 0, 0)),
+        ],
+        out_specs=pl.BlockSpec((nw, 8 * slots, LANES), lambda s: (0, 0, 0)),
+        out_shape=jax.ShapeDtypeStruct((nw, 8 * slots, LANES), jnp.bfloat16),
+        scratch_shapes=[
+            pltpu.VMEM((rows // LANES, 8 * lv * slots, LANES), jnp.float32),
+            pltpu.VMEM((lv * band // LANES, 8 * slots, LANES), jnp.float32),
+        ],
+        compiler_params=pltpu.CompilerParams(vmem_limit_bytes=VMEM_LIMIT),
+        cost_estimate=pl.CostEstimate(flops=2 * slots * band * rows * 256, bytes_accessed=2 * slots * band * rows, transcendentals=0),
+        name="inverse_legendre",
+    )(spec, legendre)
+
+
+def grid_kernel(steps, factor, recv_ref, cos_ref, sin_ref, row_ref, lane_ref, down_ref, up_ref, out_ref, operand, total):
+    i = pl.program_id(0)
+    half = recv_ref.shape[1] // 4
+    nw = recv_ref.shape[0]
+
+    @pl.when(i == 0)
+    def _():
+        for j in range(4):
+            operand[:, j * LANES : (j + 1) * LANES] = recv_ref[:, j * half : (j + 1) * half, :].reshape(nw * half, LANES)
+
+    parts = []
+    for u in range(ROWS // LANES):
+        row = row_ref[i * (ROWS // LANES) + u]
+        parts.append(cos_ref[...] * row[0:1, :] - sin_ref[...] * row[1:2, :])
+    table = jnp.concatenate(parts, axis=0)
+    values = jnp.dot(table.astype(jnp.bfloat16), operand[...], preferred_element_type=jnp.float32)
+    temper = values[:, : 2 * LANES]
+    diverg = values[:, 2 * LANES :]
+
+    def level_sum(x, matrix):
+        high = x.astype(jnp.bfloat16)
+        low = (x - high.astype(jnp.float32)).astype(jnp.bfloat16)
+        return jnp.dot(high, matrix, preferred_element_type=jnp.float32) + jnp.dot(low, matrix, preferred_element_type=jnp.float32)
+
+    geopot = level_sum(temper * lane_ref[0:1, :], up_ref[...])
+    omega = -level_sum(diverg * lane_ref[1:2, :], down_ref[...])
+    first = geopot + omega * temper
+    second = lane_ref[2:3, :] * omega + diverg * temper
+    tendency = jnp.concatenate([first, second], axis=1).astype(jnp.bfloat16)
+    part = lax.dot_general((table * factor).astype(jnp.bfloat16), tendency, (((0,), (0,)), ((), ())), preferred_element_type=jnp.float32)
+
+    @pl.when(i == 0)
+    def _():
+        total[...] = part
+
+    @pl.when(i > 0)
+    def _():
+        total[...] += part
+
+    @pl.when(i == steps - 1)
+    def _():
+        scale = lane_ref[3:4, :]
+        out_ref[...] = (total[...] * jnp.concatenate([scale, scale], axis=1)).astype(jnp.bfloat16)
+
+
+def grid_space(recv, cos_base, sin_base, row_table, lane_values, down, up):
+    steps = NLON // ROWS
+    waves = cos_base.shape[1]
+    whole = lambda a: pl.BlockSpec(a.shape, lambda i, n=a.ndim: (0,) * n)
+    args = (recv, cos_base, sin_base, row_table, lane_values, down, up)
+    return pl.pallas_call(
+        lambda *refs: grid_kernel(steps, 2.0 / NLON, *refs),
+        grid=(steps,),
+        in_specs=[whole(a) for a in args],
+        out_specs=pl.BlockSpec((waves, 4 * LANES), lambda i: (0, 0)),
+        out_shape=jax.ShapeDtypeStruct((waves, 4 * LANES), jnp.bfloat16),
+        scratch_shapes=[pltpu.VMEM((waves, 4 * LANES), jnp.bfloat16), pltpu.VMEM((waves, 4 * LANES), jnp.float32)],
+        compiler_params=pltpu.CompilerParams(vmem_limit_bytes=VMEM_LIMIT),
+        cost_estimate=pl.CostEstimate(flops=4 * NLON * waves * 4 * LANES, bytes_accessed=8 * waves * LANES, transcendentals=0),
+        name="grid_space",
+    )(*args)
+
+
+def direct_legendre_kernel(slots, lats, lv, wave_ref, recv_ref, leg_ref, out_ref, held, cut):
+    s = pl.program_id(0)
+    nw = recv_ref.shape[0]
+    blocks = leg_ref.shape[1] // LANES
+
+    @pl.when(s == 0)
+    def _():
+        for b in range(blocks):
+            total = jnp.zeros((8 * slots, lv * LANES), jnp.float32)
+            for w in range(LANES * b // lats, (LANES * (b + 1) - 1) // lats + 1):
+                first = max(lats * w, LANES * b)
+                last = min(lats * (w + 1), LANES * (b + 1))
+                x = jnp.concatenate([recv_ref[w, :, j * LANES : (j + 1) * LANES] for j in range(4)], axis=0)
+                sel = jnp.concatenate(
+                    [placed(LANES, LANES, lats * l + first - lats * w, first - LANES * b, last - first) for l in range(lv)], axis=1
+                )
+                total += jnp.dot(x, sel, preferred_element_type=jnp.float32)
+            for l in range(lv):
+                held[l * blocks + b] = total[:, l * LANES : (l + 1) * LANES]
+
+    x = jnp.concatenate(
+        [jnp.concatenate([held[l * blocks + b, pl.ds(s, 8, stride=slots), :] for b in range(blocks)], axis=1) for l in range(lv)], axis=0
+    ).astype(jnp.bfloat16)
+    y = jnp.dot(x, leg_ref[0], preferred_element_type=jnp.float32)
+    k = lax.broadcasted_iota(jnp.int32, y.shape, 1)
+    y = jnp.where(k < M - wave_ref[s], y, 0.0)
+    for b in range(cut.shape[0]):
+        cut[b, pl.ds(s, 8 * lv, stride=slots), :] = y[:, b * LANES : (b + 1) * LANES]
+
+    @pl.when(s == slots - 1)
+    def _():
+        for b in range(cut.shape[0]):
+            out_ref[:, b * LANES : (b + 1) * LANES] = cut[b]
+
+
+def direct_legendre(my_waves, recv, legendre, lv):
+    slots, band, rows = legendre.shape
+    nw = recv.shape[0]
+    return pl.pallas_call(
+        lambda *refs: direct_legendre_kernel(slots, band // nw, lv, *refs),
+        grid_spec=pltpu.PrefetchScalarGridSpec(
+            num_scalar_prefetch=1,
+            grid=(slots,),
+            in_specs=[
+                pl.BlockSpec(recv.shape, lambda s, w: (0, 0, 0)),
+                pl.BlockSpec((1, band, rows), lambda s, w: (s, 0, 0)),
+            ],
+            out_specs=pl.BlockSpec((8 * lv * slots, rows), lambda s, w: (0, 0)),
+            scratch_shapes=[
+                pltpu.VMEM((lv * band // LANES, 8 * slots, LANES), jnp.float32),
+                pltpu.VMEM((rows // LANES, 8 * lv * slots, LANES), jnp.float32),
+            ],
+        ),
+        out_shape=jax.ShapeDtypeStruct((8 * lv * slots, rows), jnp.float32),
+        compiler_params=pltpu.CompilerParams(vmem_limit_bytes=VMEM_LIMIT),
+        cost_estimate=pl.CostEstimate(flops=2 * slots * band * rows * 256, bytes_accessed=2 * slots * band * rows, transcendentals=0),
+        name="direct_legendre",
+    )(my_waves, recv, legendre)
+
+
+def body(spectral, legendre, thickness, pressure_step, wave_order, lat_order):
+    wave_index = lax.axis_index("wave")
+    lev_index = lax.axis_index("lev")
+    nw = lax.axis_size("wave")
+    slots, band, rows = legendre.shape
+    lats = band // nw
+    lv = spectral.shape[0]
+    swap = [(0, 1), (1, 0)]
+    upper = lev_index == 0
+
+    other = lax.ppermute(spectral, "lev", swap)
+    my_waves = lax.dynamic_slice(wave_order, (wave_index * slots,), (slots,))
+    in_triangle = jnp.arange(rows, dtype=jnp.int32)[None, :] < (M - my_waves)[:, None]
+    weights = jnp.where(my_waves == 0, 1.0, 2.0).astype(jnp.float32)[:, None]
+    weights = jnp.where(in_triangle, weights, 0.0)
+
+    lane_waves = jnp.broadcast_to(wave_order.reshape(nw, 1, slots), (nw, 2, slots)).reshape(1, -1)
+    turn = 2.0 * math.pi / NLON
+    inner = (lane_waves * jnp.arange(LANES, dtype=jnp.int32)[:, None] % NLON).astype(jnp.float32) * turn
+    cos_base, sin_base = jnp.cos(inner), jnp.sin(inner)
+    outer = (lane_waves * jnp.arange(0, NLON, LANES, dtype=jnp.int32)[:, None] % NLON).astype(jnp.float32) * turn
+    imaginary = (jnp.arange(2 * nw * slots) // slots % 2 == 1)[None, :]
+    cos_outer, sin_outer = jnp.cos(outer), jnp.sin(outer)
+    row_table = jnp.stack([jnp.where(imaginary, -sin_outer, cos_outer), jnp.where(imaginary, cos_outer, sin_outer)], axis=1)
+
+    lat_ids = lax.dynamic_slice(lat_order, (lev_index * band + wave_index * lats,), (lats,))
+    angles = math.pi * (lat_ids.astype(jnp.float32) + 0.75) / (NLAT + 0.5)
+
+    def lanes(by_level_lat):
+        pad = LANES - lv * lats
+        return jnp.pad(by_level_lat.reshape(2, lv * lats), ((0, 0), (0, pad))).reshape(2 * LANES)
+
+    spread = jnp.ones((2 * lv, lats), jnp.float32)
+    zero = jnp.zeros((2 * LANES,), jnp.float32)
+    lane_values = jnp.stack(
+        [lanes(thickness[:, None] * spread), lanes(pressure_step[:, None] * spread), lanes(jnp.cos(angles) * spread), lanes(jnp.sin(angles) * spread)]
+        + [zero] * 4
+    )
+    place = jnp.arange(2 * LANES)
+    valid = place % LANES < lv * lats
+    level = place // LANES * lv + place % LANES // lats
+    lat = place % LANES % lats
+    same = (lat[:, None] == lat[None, :]) & valid[:, None] & valid[None, :]
+    down = (same & (level[:, None] <= level[None, :])).astype(jnp.bfloat16)
+    up = (same & (level[:, None] >= level[None, :])).astype(jnp.bfloat16)
+
+    halves = jnp.stack([jnp.where(upper, spectral, other), jnp.where(upper, other, spectral)], axis=2)
+    spec = (halves.astype(jnp.float32) * weights).reshape(8 * lv * slots, rows)
+    sent = inverse_legendre(spec, legendre, lv, nw)
+    recv = lax.all_to_all(sent, "wave", split_axis=0, concat_axis=0, tiled=True)
+    back = grid_space(recv, cos_base, sin_base, row_table, lane_values, down, up)
+    back = lax.all_to_all(back.reshape(nw, 2 * slots, 4 * LANES), "wave", split_axis=0, concat_axis=0, tiled=True)
+    out = direct_legendre(my_waves, back, legendre, lv).reshape(lv, 2, 2, 2, slots, rows)
+    mine = jnp.where(upper, out[:, :, 0], out[:, :, 1])
+    theirs = jnp.where(upper, out[:, :, 1], out[:, :, 0]).astype(jnp.bfloat16)
+    return mine + lax.ppermute(theirs, "lev", swap).astype(jnp.float32)
+
+
 def solution(mesh):
-    in_specs = (P("lev", None, None, "wave", None), P("wave", "lev", None), P(), P(), P(), P())
-    out_specs = P("lev", None, None, "wave", None)
-    return jax.shard_map(body, mesh=mesh, in_specs=in_specs, out_specs=out_specs, check_vma=False)
+    nw, nl = mesh.shape["wave"], mesh.shape["lev"]
+
+    def run(spectral, *rest):
+        slots, lv = M // nw, spectral.shape[0] // nl
+        fits = nl == 2 and NLAT % (nw * nl) == 0 and M % nw == 0 and slots % 8 == 0
+        fits = fits and M % LANES == 0 and lv * (NLAT // (nw * nl)) <= LANES and (NLAT // nl) % LANES == 0
+        in_specs = (P("lev", None, None, "wave", None), P("wave", "lev", None), P(), P(), P(), P())
+        out_specs = P("lev", None, None, "wave", None)
+        chosen = body if fits else general_body
+        return jax.shard_map(chosen, mesh=mesh, in_specs=in_specs, out_specs=out_specs, check_vma=False)(spectral, *rest)
+
+    return run

time: 488 us -> 193 us (0.40)
  local copies, waits for them, and re-layouts: 104 us -> 1.1 us
  waiting for transfers between devices: 149 us -> 47 us
  Pallas kernels: 0 us -> 81.5 us
  blocking collectives: 119 us -> 39.3 us
  matrix products: 46 us -> 0 us
  other arithmetic: 42.2 us -> 11.2 us
  between operations: 13.6 us -> 0.18 us
    pallas_call x0 -> x3, Pallas kernels: none -> 81.5 us  [the longest x1 34.5 us: inverse_legendre(): pl.pallas_call(lambda *refs: inverse_legendre_kernel(slots, lats, lv, nw,...]
    all_to_all x4 -> x1, blocking collectives: 119 us -> 39.3 us  [body(): lax.all_to_all(back.reshape(nw, 2 * slots, 4 * LANES), 'wave', split_axis...]
    all_to_all x2 -> x1, waiting for transfers between devices: 86.5 us -> 18.8 us  [body(): recv = lax.all_to_all(sent, 'wave', split_axis=0, concat_axis=0, tiled=True)]
    all_to_all x9 -> x0, local copies, waits for them, and re-layouts: 56.2 us -> none  [the longest x2 20.9 us: body(): lax.all_to_all(grid_vals, 'lev', split_axis=3, concat_axis=0, tiled=True)]
    dot_general x4 -> x0, matrix products: 46 us -> none  [the longest x1 16.7 us: body(): jnp.einsum('lfcsk,sqk->lfcsq', lax.all_gather(spectral, 'lev', axis=0, ti...]
    another operation x5 -> x2, other arithmetic: 38.6 us -> 1.38 us  [the longest x1 1.19 us: body(): jnp.stack([jnp.where(upper, spectral, other), jnp.where(upper, other, spe...]
    reduce_scatter x1 -> x0, waiting for transfers between devices: 34.4 us -> none  [body(): lax.psum_scatter(jnp.einsum('lfcsq,sqk->lfcsk', band_vals, masked_leg, pr...]
    unnamed x16 -> x6, local copies, waits for them, and re-layouts: 29.9 us -> 0.01 us
  transfers between devices with their start and end apart: 4 -> 3, of which waited for: 3 -> 3; matrix products, arithmetic and copies ran while one was open for 7% -> 5% of each run, Pallas kernels for 0% -> 0%
where the time goes in v1:
time: 193 us; the launch traced here: 191 us
  Pallas kernels  81.5 us (42%)
  waiting for transfers between devices  47 us (24%)
  blocking collectives  39.3 us (20%)
  other arithmetic  11.2 us (6%)
  starting transfers between devices  10.8 us (6%)
    all_to_all x1, blocking collectives, body(): lax.all_to_all(back.reshape(nw, 2 * slots, 4 * LANES), 'wave', split_axis...  39.3 us
    pallas_call x1, Pallas kernels, inverse_legendre(): pl.pallas_call(lambda *refs: inverse_legendre_kernel(slots, lats, lv, nw,...  34.5 us
    pallas_call x1, Pallas kernels, direct_legendre(): pl.pallas_call(lambda *refs: direct_legendre_kernel(slots, band // nw, lv...  31.7 us
    all_to_all x1, waiting for transfers between devices, body(): recv = lax.all_to_all(sent, 'wave', split_axis=0, concat_axis=0, tiled=True)  18.8 us
    pallas_call x1, Pallas kernels, grid_space(): pl.pallas_call(lambda *refs: grid_kernel(steps, 2.0 / NLON, *refs), grid=...  15.3 us
    ppermute x1, waiting for transfers between devices, body(): return mine + lax.ppermute(theirs, 'lev', swap).astype(jnp.float32)  15 us
    ppermute x1, waiting for transfers between devices, body(): other = lax.ppermute(spectral, 'lev', swap)  13.2 us
    all_to_all x1, starting transfers between devices, body(): recv = lax.all_to_all(sent, 'wave', split_axis=0, concat_axis=0, tiled=True)  6.32 us
  transfers between devices with their start and end apart: 3, of which 3 were waited for; matrix products, arithmetic and copies ran while one was open for 5% of the time, Pallas kernels for 0%

profile of v1, /device:TPU:0, one launch (start us, length us, event | category | flops | bytes accessed | tf_op | source)
XLA Modules:
  0.0 191.1 jit_solution(5440629469293433819)
XLA Ops:
  0.0 2.9 %collective-permute-start = (bf16[3,2,2,40,640]{4,3,2,1,0:T(8,128)(2,1)}, bf16[3,2,2,40,640]{4,3,2,1,0:T(8,128)(2,1)S(1)}, u32[]{:S(2)}, u32[]{:S(2)}) collective-permute-start(bf16[3,2,2,40,640]{4,3,2,1,0:T(8,128)(2,1)} %param.6), channel_id=1, source_target_pairs={{0,1},{1,0},{2,3},{3,2},{4,5},{5,4},{6,7},{7,6},{8,9},{9,8},{10,11... | collective-permute-start | bytes 1843208 | tf_op jit(solution)/shard_map/ppermute | solution.py:290
  2.9 0.8 broadcast_subtract_fusion
  3.7 0.1 fusion.10
  3.8 13.2 %collective-permute-done = bf16[3,2,2,40,640]{4,3,2,1,0:T(8,128)(2,1)S(1)} collective-permute-done((bf16[3,2,2,40,640]{4,3,2,1,0:T(8,128)(2,1)}, bf16[3,2,2,40,640]{4,3,2,1,0:T(8,128)(2,1)S(1)}, u32[]{:S(2)}, u32[]{:S(2)}) %collective-permute-start) | collective-permute-done | bytes 614432 | tf_op jit(solution)/shard_map/ppermute | solution.py:290
  17.0 1.2 select_bitcast_fusion.1
  18.2 0.2 convert_multiply_fusion
  18.4 0.2 copy.10
  18.6 34.5 %inverse_legendre.1 = bf16[16,320,128]{2,1,0:T(8,128)(2,1)} custom-call(f32[960,640]{1,0:T(8,128)S(1)} %bitcast.33, bf16[40,640,640]{2,1,0:T(8,128)(2,1)} %refs_2_.1), custom_call_target="tpu_custom_call" | custom-call | flops 8388608000 | bytes 32768000 | tf_op jit(solution)/shard_map/inverse_legendre/pallas_call | solution.py:138
  53.1 0.0 copy-start
  53.1 0.0 copy-start.1
  53.1 0.0 copy-start.2
  53.1 6.3 %all-to-all-start = ((bf16[16,320,128]{2,1,0:T(8,128)(2,1)}), bf16[16,320,128]{2,1,0:T(8,128)(2,1)S(1)}, u32[]{:S(2)}, u32[]{:S(2)}) async-start(bf16[16,320,128]{2,1,0:T(8,128)(2,1)} %inverse_legendre.1), calls=%async_computation | async-start | bytes 2621440 | tf_op jit(solution)/shard_map/all_to_all | solution.py:329
  59.4 0.0 copy-done
  59.4 0.1 broadcast_in_dim.63
  59.5 0.1 mul.142
  59.6 0.0 copy-done.1
  59.7 0.1 mul.154
  59.7 0.1 mul.155
  59.8 0.1 mul.156
  59.9 0.0 copy-done.2
  59.9 0.1 mul.157
  60.0 0.1 mul.158
  60.1 0.1 mul.159
  60.2 0.8 fusion.21
  61.0 0.1 mul.162
  61.1 0.1 mul.164
  61.3 0.2 and_convert_fusion
  61.5 3.8 %broadcast_select_fusion.1 = (f32[20,1,1280]{2,1,0:T(1,128)S(1)}, f32[20,1,1280]{2,1,0:T(1,128)S(1)}) fusion(pred[1280]{0:T(1024)(128)(4,1)S(1)} %fusion.12, s32[20]{0:T(128)S(1)} %iota_multiply_fusion, s32[1280]{0:T(1024)S(1)} %mul.142), kind=kLoop, calls=%fused_computation.23 | loop fusion | flops 307200 | bytes 211280 | tf_op jit(solution)/shard_map/jit(_where)/select_n | solution.py:303
  65.2 0.2 pad_maximum_fusion.refs_3_
  65.4 2.6 %fusion.4 = (f32[128,1280]{1,0:T(8,128)S(1)}, f32[128,1280]{1,0:T(8,128)S(1)}) fusion(s32[1280]{0:T(1024)S(1)} %mul.142), kind=kLoop, calls=%fused_computation.11 | loop fusion | flops 1474560 | bytes 1315840 | tf_op jit(solution)/shard_map/sin | solution.py:299
  68.1 18.8 %all-to-all-done.refs_0_ = bf16[16,320,128]{2,1,0:T(8,128)(2,1)S(1)} async-done(((bf16[16,320,128]{2,1,0:T(8,128)(2,1)}), bf16[16,320,128]{2,1,0:T(8,128)(2,1)S(1)}, u32[]{:S(2)}, u32[]{:S(2)}) %all-to-all-start) | async-done | bytes 1310752 | tf_op jit(solution)/shard_map/all_to_all | solution.py:329
  86.8 15.3 %grid_space.1 = bf16[1280,512]{1,0:T(8,128)(2,1)S(1)} custom-call(bf16[16,320,128]{2,1,0:T(8,128)(2,1)S(1)} %all-to-all-done.refs_0_, f32[128,1280]{1,0:T(8,128)S(1)} %get-tuple-element.14.refs_1_, f32[128,1280]{1,0:T(8,128)S(1)} %get-tuple-element.13.refs_2_, f32[20,2,1280]{2,1,0:T(2,128)S(1)} %pad_maximum_fusion.refs_3_, f32[8,256]{1,0:T(8,128)S(1)} %stack.25.refs_4_, ...), custom_call_target="tpu_custom_call" | custom-call | flops 6710886400 | bytes 1310720 | tf_op jit(solution)/shard_map/grid_space/pallas_call | solution.py:207
  102.1 39.3 %all_to_all.10.refs_1_ = bf16[16,80,512]{2,1,0:T(8,128)(2,1)S(1)} all-to-all(bf16[16,80,512]{2,1,0:T(8,128)(2,1)S(1)} %bitcast.34), channel_id=1, replica_groups=mesh['wave'=16,'lev'=2] {'wave'}, dimensions={0} | all-to-all | bytes 2621440 | tf_op jit(solution)/shard_map/all_to_all | solution.py:331
  141.4 31.7 %direct_legendre.1 = f32[960,640]{1,0:T(8,128)S(1)} custom-call(s32[40]{0:T(128)S(1)} %get-tuple-element.6.refs_0_, bf16[16,80,512]{2,1,0:T(8,128)(2,1)S(1)} %all_to_all.10.refs_1_, bf16[40,640,640]{2,1,0:T(8,128)(2,1)} %refs_2_.1), custom_call_target="tpu_custom_call" | custom-call | flops 8388608000 | bytes 32768000 | tf_op jit(solution)/shard_map/direct_legendre/pallas_call | solution.py:258
  173.2 0.1 fusion.7
  173.3 1.6 collective-permute-start.1
  174.9 15.0 %collective-permute-done.1 = bf16[3,2,2,40,640]{4,3,2,1,0:T(8,128)(2,1)S(1)} collective-permute-done((bf16[3,2,2,40,640]{4,3,2,1,0:T(8,128)(2,1)S(1)}, bf16[3,2,2,40,640]{4,3,2,1,0:T(8,128)(2,1)S(1)}, u32[]{:S(2)}, u32[]{:S(2)}) %collective-permute-start.1) | collective-permute-done | bytes 614432 | tf_op jit(solution)/shard_map/ppermute | solution.py:335
  189.9 1.2 bitcast_add_fusion
  (16 shorter events, 0.1 us)
Async XLA Ops:
  0.0 17.0 %collective-permute-start = (bf16[3,2,2,40,640]{4,3,2,1,0:T(8,128)(2,1)}, bf16[3,2,2,40,640]{4,3,2,1,0:T(8,128)(2,1)S(1)}, u32[]{:S(2)}, u32[]{:S(2)}) collective-permute-start(bf16[3,2,2,40,640]{4,3,2,1,0:T(8,128)(2,1)} %param.6), channel_id=1, source_target_pairs={{0,1},{1,0},{2,3},{3,2},{4,5},{5,4},{6,7},{7,6},{8,9},{9,8},{10,11... | collective-permute-start | bytes 1843208 | tf_op jit(solution)/shard_map/ppermute | solution.py:290
  53.1 6.3 %copy-start = (s32[640]{0:T(1024)S(1)}, s32[640]{0:T(1024)}, u32[]{:S(2)}) copy-start(s32[640]{0:T(1024)} %param.10) | copy-start | bytes 7684
  53.1 6.5 %copy-start.1 = (f32[6]{0:T(128)S(1)}, f32[6]{0:T(128)}, u32[]{:S(2)}) copy-start(f32[6]{0:T(128)} %param.8) | copy-start | bytes 76
  53.1 6.8 %copy-start.2 = (f32[6]{0:T(128)S(1)}, f32[6]{0:T(128)}, u32[]{:S(2)}) copy-start(f32[6]{0:T(128)} %param.9) | copy-start | bytes 76
  53.1 33.7 %all-to-all-start = ((bf16[16,320,128]{2,1,0:T(8,128)(2,1)}), bf16[16,320,128]{2,1,0:T(8,128)(2,1)S(1)}, u32[]{:S(2)}, u32[]{:S(2)}) async-start(bf16[16,320,128]{2,1,0:T(8,128)(2,1)} %inverse_legendre.1), calls=%async_computation | async-start | bytes 2621440 | tf_op jit(solution)/shard_map/all_to_all | solution.py:329
  173.3 16.6 %collective-permute-start.1 = (bf16[3,2,2,40,640]{4,3,2,1,0:T(8,128)(2,1)S(1)}, bf16[3,2,2,40,640]{4,3,2,1,0:T(8,128)(2,1)S(1)}, u32[]{:S(2)}, u32[]{:S(2)}) collective-permute-start(bf16[3,2,2,40,640]{4,3,2,1,0:T(8,128)(2,1)S(1)} %fusion.7), channel_id=1, source_target_pairs={{0,1},{1,0},{2,3},{3,2},{4,5},{5,4},{6,7},{7,6},{8,9},{9,8},{10,11... | collective-permute-start | bytes 1843208 | tf_op jit(solution)/shard_map/ppermute | solution.py:335

commit v2 on v1

--- a/solution.py
+++ b/solution.py
@@ -93,6 +93,7 @@
 
 LANES = 128
 ROWS = 256
+UNROLL = 4
 VMEM_LIMIT = 48 * 1024 * 1024
 
 
@@ -104,22 +105,30 @@
 
 
 def inverse_legendre_kernel(slots, lats, lv, nw, spec_ref, leg_ref, out_ref, cut, held):
-    s = pl.program_id(0)
+    step = pl.program_id(0)
     tiles = cut.shape[0]
-
-    @pl.when(s == 0)
+    count = 8 * lv
+
+    @pl.when(step == 0)
     def _():
         for b in range(tiles):
             cut[b] = spec_ref[:, b * LANES : (b + 1) * LANES]
 
-    x = jnp.concatenate([cut[b, pl.ds(s, 8 * lv, stride=slots), :] for b in range(tiles)], axis=1).astype(jnp.bfloat16)
-    y = lax.dot_general(x, leg_ref[0], (((1,), (1,)), ((), ())), preferred_element_type=jnp.float32)
+    total = None
+    for j in range(UNROLL):
+        x = jnp.concatenate([cut[b, pl.ds(step * UNROLL + j, count, stride=slots), :] for b in range(tiles)], axis=1)
+        x = jnp.concatenate([x if i == j else jnp.zeros_like(x) for i in range(UNROLL)], axis=0).astype(jnp.bfloat16)
+        part = lax.dot_general(leg_ref[j], x, (((1,), (1,)), ((), ())), preferred_element_type=jnp.float32)
+        total = part if total is None else total + part
+    y = total.T
     blocks = y.shape[1] // LANES
-    for l in range(lv):
-        for b in range(blocks):
-            held[l * blocks + b, pl.ds(s, 8, stride=slots), :] = y[8 * l : 8 * l + 8, b * LANES : (b + 1) * LANES]
-
-    @pl.when(s == slots - 1)
+    for j in range(UNROLL):
+        for l in range(lv):
+            for b in range(blocks):
+                r = count * j + 8 * l
+                held[l * blocks + b, pl.ds(step * UNROLL + j, 8, stride=slots), :] = y[r : r + 8, b * LANES : (b + 1) * LANES]
+
+    @pl.when(step == slots // UNROLL - 1)
     def _():
         for d in range(nw):
             total = jnp.zeros((8 * slots, LANES), jnp.float32)
@@ -132,15 +141,15 @@
             out_ref[d] = total.astype(jnp.bfloat16)
 
 
-def inverse_legendre(spec, legendre, lv, nw):
-    slots, band, rows = legendre.shape
+def inverse_legendre(spec, legendre, start, slots, lv, nw):
+    _, band, rows = legendre.shape
     lats = band // nw
     return pl.pallas_call(
         lambda *refs: inverse_legendre_kernel(slots, lats, lv, nw, *refs),
-        grid=(slots,),
+        grid=(slots // UNROLL,),
         in_specs=[
             pl.BlockSpec((8 * lv * slots, rows), lambda s: (0, 0)),
-            pl.BlockSpec((1, band, rows), lambda s: (s, 0, 0)),
+            pl.BlockSpec((UNROLL, band, rows), lambda s: (s + start // UNROLL, 0, 0)),
         ],
         out_specs=pl.BlockSpec((nw, 8 * slots, LANES), lambda s: (0, 0, 0)),
         out_shape=jax.ShapeDtypeStruct((nw, 8 * slots, LANES), jnp.bfloat16),
@@ -154,15 +163,19 @@
     )(spec, legendre)
 
 
-def grid_kernel(steps, factor, recv_ref, cos_ref, sin_ref, row_ref, lane_ref, down_ref, up_ref, out_ref, operand, total):
+def grid_kernel(steps, factor, groups, *refs):
     i = pl.program_id(0)
-    half = recv_ref.shape[1] // 4
-    nw = recv_ref.shape[0]
+    recvs, (cos_ref, sin_ref, row_ref, lane_ref, down_ref, up_ref) = refs[:groups], refs[groups : groups + 6]
+    outs, (operand, total) = refs[groups + 6 : -2], refs[-2:]
 
     @pl.when(i == 0)
     def _():
-        for j in range(4):
-            operand[:, j * LANES : (j + 1) * LANES] = recv_ref[:, j * half : (j + 1) * half, :].reshape(nw * half, LANES)
+        top = 0
+        for recv in recvs:
+            nw, half = recv.shape[0], recv.shape[1] // 4
+            for j in range(4):
+                operand[top : top + nw * half, j * LANES : (j + 1) * LANES] = recv[:, j * half : (j + 1) * half, :].reshape(nw * half, LANES)
+            top += nw * half
 
     parts = []
     for u in range(ROWS // LANES):
@@ -196,20 +209,28 @@
     @pl.when(i == steps - 1)
     def _():
         scale = lane_ref[3:4, :]
-        out_ref[...] = (total[...] * jnp.concatenate([scale, scale], axis=1)).astype(jnp.bfloat16)
-
-
-def grid_space(recv, cos_base, sin_base, row_table, lane_values, down, up):
+        scale = jnp.concatenate([scale, scale], axis=1)
+        top = 0
+        for out in outs:
+            nw, half = out.shape[0], out.shape[1] // 4
+            for j in range(4):
+                lanes = slice(j * LANES, (j + 1) * LANES)
+                block = (total[top : top + nw * half, lanes] * scale[:, lanes]).astype(jnp.bfloat16)
+                out[:, j * half : (j + 1) * half, :] = block.reshape(nw, half, LANES)
+            top += nw * half
+
+
+def grid_space(recvs, *tables):
     steps = NLON // ROWS
-    waves = cos_base.shape[1]
+    waves = tables[0].shape[1]
     whole = lambda a: pl.BlockSpec(a.shape, lambda i, n=a.ndim: (0,) * n)
-    args = (recv, cos_base, sin_base, row_table, lane_values, down, up)
+    args = (*recvs, *tables)
     return pl.pallas_call(
-        lambda *refs: grid_kernel(steps, 2.0 / NLON, *refs),
+        lambda *refs: grid_kernel(steps, 2.0 / NLON, len(recvs), *refs),
         grid=(steps,),
         in_specs=[whole(a) for a in args],
-        out_specs=pl.BlockSpec((waves, 4 * LANES), lambda i: (0, 0)),
-        out_shape=jax.ShapeDtypeStruct((waves, 4 * LANES), jnp.bfloat16),
+        out_specs=[whole(a) for a in recvs],
+        out_shape=[jax.ShapeDtypeStruct(a.shape, a.dtype) for a in recvs],
         scratch_shapes=[pltpu.VMEM((waves, 4 * LANES), jnp.bfloat16), pltpu.VMEM((waves, 4 * LANES), jnp.float32)],
         compiler_params=pltpu.CompilerParams(vmem_limit_bytes=VMEM_LIMIT),
         cost_estimate=pl.CostEstimate(flops=4 * NLON * waves * 4 * LANES, bytes_accessed=8 * waves * LANES, transcendentals=0),
@@ -217,52 +238,52 @@
     )(*args)
 
 
-def direct_legendre_kernel(slots, lats, lv, wave_ref, recv_ref, leg_ref, out_ref, held, cut):
-    s = pl.program_id(0)
-    nw = recv_ref.shape[0]
+def direct_legendre_kernel(start, slots, lats, lv, wave_ref, recv_ref, leg_ref, out_ref, held, cut):
+    step = pl.program_id(0)
     blocks = leg_ref.shape[1] // LANES
 
-    @pl.when(s == 0)
+    @pl.when(step == 0)
     def _():
         for b in range(blocks):
             total = jnp.zeros((8 * slots, lv * LANES), jnp.float32)
             for w in range(LANES * b // lats, (LANES * (b + 1) - 1) // lats + 1):
                 first = max(lats * w, LANES * b)
                 last = min(lats * (w + 1), LANES * (b + 1))
-                x = jnp.concatenate([recv_ref[w, :, j * LANES : (j + 1) * LANES] for j in range(4)], axis=0)
                 sel = jnp.concatenate(
                     [placed(LANES, LANES, lats * l + first - lats * w, first - LANES * b, last - first) for l in range(lv)], axis=1
                 )
-                total += jnp.dot(x, sel, preferred_element_type=jnp.float32)
+                total += jnp.dot(recv_ref[w], sel, preferred_element_type=jnp.float32)
             for l in range(lv):
                 held[l * blocks + b] = total[:, l * LANES : (l + 1) * LANES]
 
-    x = jnp.concatenate(
-        [jnp.concatenate([held[l * blocks + b, pl.ds(s, 8, stride=slots), :] for b in range(blocks)], axis=1) for l in range(lv)], axis=0
-    ).astype(jnp.bfloat16)
-    y = jnp.dot(x, leg_ref[0], preferred_element_type=jnp.float32)
-    k = lax.broadcasted_iota(jnp.int32, y.shape, 1)
-    y = jnp.where(k < M - wave_ref[s], y, 0.0)
-    for b in range(cut.shape[0]):
-        cut[b, pl.ds(s, 8 * lv, stride=slots), :] = y[:, b * LANES : (b + 1) * LANES]
-
-    @pl.when(s == slots - 1)
+    for j in range(UNROLL):
+        s = step * UNROLL + j
+        x = jnp.concatenate(
+            [jnp.concatenate([held[l * blocks + b, pl.ds(s, 8, stride=slots), :] for b in range(blocks)], axis=1) for l in range(lv)], axis=0
+        ).astype(jnp.bfloat16)
+        y = jnp.dot(x, leg_ref[j], preferred_element_type=jnp.float32)
+        k = lax.broadcasted_iota(jnp.int32, y.shape, 1)
+        y = jnp.where(k < M - wave_ref[start + s], y, 0.0)
+        for b in range(cut.shape[0]):
+            cut[b, pl.ds(s, 8 * lv, stride=slots), :] = y[:, b * LANES : (b + 1) * LANES]
+
+    @pl.when(step == slots // UNROLL - 1)
     def _():
         for b in range(cut.shape[0]):
             out_ref[:, b * LANES : (b + 1) * LANES] = cut[b]
 
 
-def direct_legendre(my_waves, recv, legendre, lv):
-    slots, band, rows = legendre.shape
+def direct_legendre(my_waves, recv, legendre, start, slots, lv):
+    _, band, rows = legendre.shape
     nw = recv.shape[0]
     return pl.pallas_call(
-        lambda *refs: direct_legendre_kernel(slots, band // nw, lv, *refs),
+        lambda *refs: direct_legendre_kernel(start, slots, band // nw, lv, *refs),
         grid_spec=pltpu.PrefetchScalarGridSpec(
             num_scalar_prefetch=1,
-            grid=(slots,),
+            grid=(slots // UNROLL,),
             in_specs=[
                 pl.BlockSpec(recv.shape, lambda s, w: (0, 0, 0)),
-                pl.BlockSpec((1, band, rows), lambda s, w: (s, 0, 0)),
+                pl.BlockSpec((UNROLL, band, rows), lambda s, w: (s + start // UNROLL, 0, 0)),
             ],
             out_specs=pl.BlockSpec((8 * lv * slots, rows), lambda s, w: (0, 0)),
             scratch_shapes=[
@@ -287,18 +308,24 @@
     swap = [(0, 1), (1, 0)]
     upper = lev_index == 0
 
-    other = lax.ppermute(spectral, "lev", swap)
+    cutoff = slots * 2 // 5 // 8 * 8
+    groups = [(0, cutoff), (cutoff, slots - cutoff)] if cutoff else [(0, slots)]
+    own = [spectral[:, :, :, start : start + n] for start, n in groups]
+    others = [lax.ppermute(x, "lev", swap) for x in own]
     my_waves = lax.dynamic_slice(wave_order, (wave_index * slots,), (slots,))
     in_triangle = jnp.arange(rows, dtype=jnp.int32)[None, :] < (M - my_waves)[:, None]
     weights = jnp.where(my_waves == 0, 1.0, 2.0).astype(jnp.float32)[:, None]
     weights = jnp.where(in_triangle, weights, 0.0)
 
-    lane_waves = jnp.broadcast_to(wave_order.reshape(nw, 1, slots), (nw, 2, slots)).reshape(1, -1)
+    by_device = wave_order.reshape(nw, 1, slots)
+    lane_waves = jnp.concatenate(
+        [jnp.broadcast_to(by_device[:, :, start : start + n], (nw, 2, n)).reshape(1, -1) for start, n in groups], axis=1
+    )
+    imaginary = jnp.concatenate([jnp.arange(2 * nw * n) // n % 2 == 1 for _, n in groups])[None, :]
     turn = 2.0 * math.pi / NLON
     inner = (lane_waves * jnp.arange(LANES, dtype=jnp.int32)[:, None] % NLON).astype(jnp.float32) * turn
     cos_base, sin_base = jnp.cos(inner), jnp.sin(inner)
     outer = (lane_waves * jnp.arange(0, NLON, LANES, dtype=jnp.int32)[:, None] % NLON).astype(jnp.float32) * turn
-    imaginary = (jnp.arange(2 * nw * slots) // slots % 2 == 1)[None, :]
     cos_outer, sin_outer = jnp.cos(outer), jnp.sin(outer)
     row_table = jnp.stack([jnp.where(imaginary, -sin_outer, cos_outer), jnp.where(imaginary, cos_outer, sin_outer)], axis=1)
 
@@ -323,16 +350,21 @@
     down = (same & (level[:, None] <= level[None, :])).astype(jnp.bfloat16)
     up = (same & (level[:, None] >= level[None, :])).astype(jnp.bfloat16)
 
-    halves = jnp.stack([jnp.where(upper, spectral, other), jnp.where(upper, other, spectral)], axis=2)
-    spec = (halves.astype(jnp.float32) * weights).reshape(8 * lv * slots, rows)
-    sent = inverse_legendre(spec, legendre, lv, nw)
-    recv = lax.all_to_all(sent, "wave", split_axis=0, concat_axis=0, tiled=True)
-    back = grid_space(recv, cos_base, sin_base, row_table, lane_values, down, up)
-    back = lax.all_to_all(back.reshape(nw, 2 * slots, 4 * LANES), "wave", split_axis=0, concat_axis=0, tiled=True)
-    out = direct_legendre(my_waves, back, legendre, lv).reshape(lv, 2, 2, 2, slots, rows)
-    mine = jnp.where(upper, out[:, :, 0], out[:, :, 1])
-    theirs = jnp.where(upper, out[:, :, 1], out[:, :, 0]).astype(jnp.bfloat16)
-    return mine + lax.ppermute(theirs, "lev", swap).astype(jnp.float32)
+    recvs = []
+    for (start, n), x, other in zip(groups, own, others):
+        halves = jnp.stack([jnp.where(upper, x, other), jnp.where(upper, other, x)], axis=2)
+        spec = (halves.astype(jnp.float32) * weights[start : start + n]).reshape(8 * lv * n, rows)
+        sent = inverse_legendre(spec, legendre, start, n, lv, nw)
+        recvs.append(lax.all_to_all(sent, "wave", split_axis=0, concat_axis=0, tiled=True))
+    backs = grid_space(recvs, cos_base, sin_base, row_table, lane_values, down, up)
+    results = []
+    for (start, n), back in reversed(list(zip(groups, backs))):
+        back = lax.all_to_all(back, "wave", split_axis=0, concat_axis=0, tiled=True)
+        out = direct_legendre(my_waves, back, legendre, start, n, lv).reshape(lv, 2, 2, 2, n, rows)
+        mine = jnp.where(upper, out[:, :, 0], out[:, :, 1])
+        theirs = jnp.where(upper, out[:, :, 1], out[:, :, 0]).astype(jnp.bfloat16)
+        results.append(mine + lax.ppermute(theirs, "lev", swap).astype(jnp.float32))
+    return jnp.concatenate(results[::-1], axis=3)
 
 
 def solution(mesh):

time: 193 us -> 147 us (0.76)
  Pallas kernels: 81.5 us -> 55.9 us
  blocking collectives: 39.3 us -> 19.7 us
  waiting for transfers between devices: 47 us -> 35 us
  starting transfers between devices: 10.8 us -> 21.3 us
  local copies, waits for them, and re-layouts: 1.1 us -> 3.34 us
    all_to_all x1, blocking collectives: 39.3 us -> 19.7 us  [body(): back = lax.all_to_all(back, 'wave', split_axis=0, concat_axis=0, tiled=True)]
    ppermute x2 -> x4, waiting for transfers between devices: 28.3 us -> 13.1 us  [the longest x2 9.21 us: body(): results.append(mine + lax.ppermute(theirs, 'lev', swap).astype(jnp.float32))]
    pallas_call x1 -> x2, Pallas kernels: 34.5 us -> 21.4 us  [inverse_legendre(): pl.pallas_call(lambda *refs: inverse_legendre_kernel(slots, lats, lv, nw,...]
    pallas_call x2 -> x3, Pallas kernels: 47 us -> 34.6 us  [the longest x2 18.3 us: direct_legendre(): pl.pallas_call(lambda *refs: direct_legendre_kernel(start, slots, band //...]
    all_to_all x1 -> x3, starting transfers between devices: 6.32 us -> 15.2 us  [the longest x2 11.1 us: body(): lax.all_to_all(sent, 'wave', split_axis=0, concat_axis=0, tiled=True)]
    all_to_all x1 -> x3, waiting for transfers between devices: 18.8 us -> 21.9 us  [the longest x2 12.4 us: body(): lax.all_to_all(sent, 'wave', split_axis=0, concat_axis=0, tiled=True)]
    slice x0 -> x6, local copies, waits for them, and re-layouts: none -> 2.15 us  [the longest x2 2.06 us: body(): own = [spectral[:, :, :, start:start + n] for start, n in groups]]
    ppermute x2 -> x4, starting transfers between devices: 4.49 us -> 6.16 us  [the longest x2 3.09 us: body(): others = [lax.ppermute(x, 'lev', swap) for x in own]]
  transfers between devices with their start and end apart: 3 -> 7, of which waited for: 3 -> 5; matrix products, arithmetic and copies ran while one was open for 5% -> 8% of each run, Pallas kernels for 0% -> 27%
where the time goes in v2:
time: 147 us; the launch traced here: 146 us
  Pallas kernels  55.9 us (38%)
  waiting for transfers between devices  35 us (24%)
  starting transfers between devices  21.3 us (14%)
  blocking collectives  19.7 us (13%)
  other arithmetic  10.3 us (7%)
  local copies, waits for them, and re-layouts  3.34 us (2%)
    pallas_call x2, Pallas kernels, inverse_legendre(): pl.pallas_call(lambda *refs: inverse_legendre_kernel(slots, lats, lv, nw,...  21.4 us
    all_to_all x1, blocking collectives, body(): back = lax.all_to_all(back, 'wave', split_axis=0, concat_axis=0, tiled=True)  19.7 us
    pallas_call x2, Pallas kernels, direct_legendre(): pl.pallas_call(lambda *refs: direct_legendre_kernel(start, slots, band //...  18.3 us
    pallas_call x1, Pallas kernels, grid_space(): pl.pallas_call(lambda *refs: grid_kernel(steps, 2.0 / NLON, len(recvs), *...  16.3 us
    all_to_all x2, waiting for transfers between devices, body(): lax.all_to_all(sent, 'wave', split_axis=0, concat_axis=0, tiled=True)  12.4 us
    all_to_all x2, starting transfers between devices, body(): lax.all_to_all(sent, 'wave', split_axis=0, concat_axis=0, tiled=True)  11.1 us
    all_to_all x1, waiting for transfers between devices, body(): back = lax.all_to_all(back, 'wave', split_axis=0, concat_axis=0, tiled=True)  9.43 us
    ppermute x2, waiting for transfers between devices, body(): results.append(mine + lax.ppermute(theirs, 'lev', swap).astype(jnp.float32))  9.21 us
  transfers between devices with their start and end apart: 7, of which 5 were waited for; matrix products, arithmetic and copies ran while one was open for 8% of the time, Pallas kernels for 27%

profile of v2, /device:TPU:0, one launch (start us, length us, event | category | flops | bytes accessed | tf_op | source)
XLA Modules:
  0.0 145.9 jit_solution(3523321157688228574)
XLA Ops:
  0.0 0.0 copy-start
  0.0 1.0 slice.34
  1.0 3.0 %collective-permute-start = (bf16[3,2,2,16,640]{4,3,2,1,0:T(8,128)(2,1)S(1)}, bf16[3,2,2,16,640]{4,3,2,1,0:T(8,128)(2,1)S(1)}, u32[]{:S(2)}, u32[]{:S(2)}) collective-permute-start(bf16[3,2,2,16,640]{4,3,2,1,0:T(8,128)(2,1)S(1)} %slice.34), channel_id=1, source_target_pairs={{0,1},{1,0},{2,3},{3,2},{4,5},{5,4},{6,7},{7,6},{8,9},{9,8},{10,11... | collective-permute-start | bytes 737288 | tf_op jit(solution)/shard_map/ppermute | solution.py:314
  4.0 1.0 slice.36
  5.1 0.1 collective-permute-start.1
  5.2 0.8 broadcast_subtract_fusion
  6.0 0.8 fusion.27
  6.8 0.1 fusion.11
  6.9 0.0 copy-start.1
  6.9 3.9 %collective-permute-done = bf16[3,2,2,16,640]{4,3,2,1,0:T(8,128)(2,1)S(1)} collective-permute-done((bf16[3,2,2,16,640]{4,3,2,1,0:T(8,128)(2,1)S(1)}, bf16[3,2,2,16,640]{4,3,2,1,0:T(8,128)(2,1)S(1)}, u32[]{:S(2)}, u32[]{:S(2)}) %collective-permute-start) | collective-permute-done | bytes 245792 | tf_op jit(solution)/shard_map/ppermute | solution.py:314
  10.8 0.0 copy-done
  10.8 0.1 select_bitcast_fusion.3
  10.9 0.1 convert_multiply_fusion.1
  11.0 0.1 copy.13
  11.1 0.0 copy-done.1
  11.1 9.0 %inverse_legendre.2 = bf16[16,128,128]{2,1,0:T(8,128)(2,1)} custom-call(f32[384,640]{1,0:T(8,128)S(1)} %bitcast.64, bf16[40,640,640]{2,1,0:T(8,128)(2,1)} %refs_2_.3), custom_call_target="tpu_custom_call" | custom-call | flops 3355443200 | bytes 13107200 | tf_op jit(solution)/shard_map/inverse_legendre/pallas_call | solution.py:147
  20.0 0.0 slice-start
  20.0 6.6 %all-to-all-start = ((bf16[16,128,128]{2,1,0:T(8,128)(2,1)}), bf16[16,128,128]{2,1,0:T(8,128)(2,1)S(1)}, u32[]{:S(2)}, u32[]{:S(2)}) async-start(bf16[16,128,128]{2,1,0:T(8,128)(2,1)} %inverse_legendre.2), calls=%async_computation | async-start | bytes 1048576 | tf_op jit(solution)/shard_map/all_to_all | solution.py:358
  26.7 0.0 collective-permute-done.1
  26.7 0.1 select_bitcast_fusion.1
  26.8 0.0 slice-done
  26.8 0.1 convert_multiply_fusion
  26.9 0.1 copy.14
  27.0 12.4 %inverse_legendre.3 = bf16[16,192,128]{2,1,0:T(8,128)(2,1)} custom-call(f32[576,640]{1,0:T(8,128)S(1)} %bitcast.63, bf16[40,640,640]{2,1,0:T(8,128)(2,1)} %refs_2_.3), custom_call_target="tpu_custom_call" | custom-call | flops 5033164800 | bytes 19660800 | tf_op jit(solution)/shard_map/inverse_legendre/pallas_call | solution.py:147
  39.4 0.0 copy-start.2
  39.4 0.0 copy-start.3
  39.4 0.0 copy-start.4
  39.4 1.7 %all-to-all-done.refs_0_ = bf16[16,128,128]{2,1,0:T(8,128)(2,1)S(1)} async-done(((bf16[16,128,128]{2,1,0:T(8,128)(2,1)}), bf16[16,128,128]{2,1,0:T(8,128)(2,1)S(1)}, u32[]{:S(2)}, u32[]{:S(2)}) %all-to-all-start) | async-done | bytes 524320 | tf_op jit(solution)/shard_map/all_to_all | solution.py:358
  41.1 4.4 %all-to-all-start.1 = ((bf16[16,192,128]{2,1,0:T(8,128)(2,1)}), bf16[16,192,128]{2,1,0:T(8,128)(2,1)S(1)}, u32[]{:S(2)}, u32[]{:S(2)}) async-start(bf16[16,192,128]{2,1,0:T(8,128)(2,1)} %inverse_legendre.3), calls=%async_computation.1 | async-start | bytes 1572864 | tf_op jit(solution)/shard_map/all_to_all | solution.py:358
  45.6 0.0 copy-done.2
  45.6 0.1 reshape.299
  45.7 0.0 copy-done.3
  45.7 0.1 mul.169
  45.8 0.0 copy-done.4
  45.8 0.1 mul.172
  45.9 0.1 mul.179
  46.0 0.1 mul.177
  46.1 0.1 mul.173
  46.1 0.1 mul.174
  46.2 0.1 mul.170
  46.3 0.1 mul.171
  46.4 0.1 slice.47
  46.5 0.1 reshape.301
  46.6 0.1 reshape.300
  46.8 0.2 and_convert_fusion
  47.0 3.8 %broadcast_select_fusion.1 = (f32[20,1,1280]{2,1,0:T(1,128)S(1)}, f32[20,1,1280]{2,1,0:T(1,128)S(1)}) fusion(pred[1280]{0:T(1024)(128)(4,1)S(1)} %pad_add_fusion, s32[20]{0:T(128)S(1)} %iota_multiply_fusion, s32[1280]{0:T(1024)S(1)} %add_reduce_fusion), kind=kLoop, calls=%fused_computation.32 | loop fusion | flops 307200 | bytes 211280 | tf_op jit(solution)/shard_map/jit(_where)/select_n | solution.py:330
  50.8 0.2 pad_maximum_fusion.1.refs_4_
  50.9 2.6 %fusion.4 = (f32[128,1280]{1,0:T(8,128)S(1)}, f32[128,1280]{1,0:T(8,128)S(1)}) fusion(s32[1280]{0:T(1024)S(1)} %add_reduce_fusion), kind=kLoop, calls=%fused_computation.13 | loop fusion | flops 1474560 | bytes 1315840 | tf_op jit(solution)/shard_map/sin | solution.py:327
  53.6 10.7 %all-to-all-done.1.refs_1_ = bf16[16,192,128]{2,1,0:T(8,128)(2,1)S(1)} async-done(((bf16[16,192,128]{2,1,0:T(8,128)(2,1)}), bf16[16,192,128]{2,1,0:T(8,128)(2,1)S(1)}, u32[]{:S(2)}, u32[]{:S(2)}) %all-to-all-start.1) | async-done | bytes 786464 | tf_op jit(solution)/shard_map/all_to_all | solution.py:358
  64.3 16.3 %grid_space.1 = (bf16[16,128,128]{2,1,0:T(8,128)(2,1)S(1)}, bf16[16,192,128]{2,1,0:T(8,128)(2,1)}) custom-call(bf16[16,128,128]{2,1,0:T(8,128)(2,1)S(1)} %all-to-all-done.refs_0_, bf16[16,192,128]{2,1,0:T(8,128)(2,1)S(1)} %all-to-all-done.1.refs_1_, f32[128,1280]{1,0:T(8,128)S(1)} %get-tuple-element.20.refs_2_, f32[128,1280]{1,0:T(8,128)S(1)} %get-tuple-element.19.refs_3_, ...), custom_call_target="tpu_custom_call" | custom-call | flops 6710886400 | bytes 1310720 | tf_op jit(solution)/shard_map/grid_space/pallas_call | solution.py:228
  80.6 19.7 %all_to_all.20.refs_1_ = bf16[16,128,128]{2,1,0:T(8,128)(2,1)S(1)} all-to-all(bf16[16,128,128]{2,1,0:T(8,128)(2,1)S(1)} %get-tuple-element.7), channel_id=1, replica_groups=mesh['wave'=16,'lev'=2] {'wave'}, dimensions={0} | all-to-all | bytes 1048576 | tf_op jit(solution)/shard_map/all_to_all | solution.py:362
  100.3 4.1 %all-to-all-start.3 = ((bf16[16,192,128]{2,1,0:T(8,128)(2,1)}), bf16[16,192,128]{2,1,0:T(8,128)(2,1)S(1)}, u32[]{:S(2)}, u32[]{:S(2)}) async-start(bf16[16,192,128]{2,1,0:T(8,128)(2,1)} %get-tuple-element.8), calls=%async_computation.3 | async-start | bytes 1572864 | tf_op jit(solution)/shard_map/all_to_all | solution.py:362
  104.4 7.7 %direct_legendre.2 = f32[384,640]{1,0:T(8,128)S(1)} custom-call(s32[40]{0:T(128)S(1)} %get-tuple-element.10.refs_0_, bf16[16,128,128]{2,1,0:T(8,128)(2,1)S(1)} %all_to_all.20.refs_1_, bf16[40,640,640]{2,1,0:T(8,128)(2,1)} %refs_2_.3), custom_call_target="tpu_custom_call" | custom-call | flops 3355443200 | bytes 13107200 | tf_op jit(solution)/shard_map/direct_legendre/pallas_call | solution.py:279
  112.1 0.1 fusion.8
  112.2 1.5 %collective-permute-start.2 = (bf16[3,2,2,16,640]{4,3,2,1,0:T(8,128)(2,1)S(1)}, bf16[3,2,2,16,640]{4,3,2,1,0:T(8,128)(2,1)S(1)}, u32[]{:S(2)}, u32[]{:S(2)}) collective-permute-start(bf16[3,2,2,16,640]{4,3,2,1,0:T(8,128)(2,1)S(1)} %fusion.8), channel_id=1, source_target_pairs={{0,1},{1,0},{2,3},{3,2},{4,5},{5,4},{6,7},{7,6},{8,9},{9,8},{10,11... | collective-permute-start | bytes 737288 | tf_op jit(solution)/shard_map/ppermute | solution.py:366
  113.7 9.4 %all-to-all-done.3.refs_1_ = bf16[16,192,128]{2,1,0:T(8,128)(2,1)S(1)} async-done(((bf16[16,192,128]{2,1,0:T(8,128)(2,1)}), bf16[16,192,128]{2,1,0:T(8,128)(2,1)S(1)}, u32[]{:S(2)}, u32[]{:S(2)}) %all-to-all-start.3) | async-done | bytes 786464 | tf_op jit(solution)/shard_map/all_to_all | solution.py:362
  123.2 10.6 %direct_legendre.3 = f32[576,640]{1,0:T(8,128)S(1)} custom-call(s32[40]{0:T(128)S(1)} %get-tuple-element.10.refs_0_, bf16[16,192,128]{2,1,0:T(8,128)(2,1)S(1)} %all-to-all-done.3.refs_1_, bf16[40,640,640]{2,1,0:T(8,128)(2,1)} %refs_2_.3), custom_call_target="tpu_custom_call" | custom-call | flops 5033164800 | bytes 19660800 | tf_op jit(solution)/shard_map/direct_legendre/pallas_call | solution.py:279
  133.8 0.1 fusion.7
  133.9 1.5 %collective-permute-start.3 = (bf16[3,2,2,24,640]{4,3,2,1,0:T(8,128)(2,1)S(1)}, bf16[3,2,2,24,640]{4,3,2,1,0:T(8,128)(2,1)S(1)}, u32[]{:S(2)}, u32[]{:S(2)}) collective-permute-start(bf16[3,2,2,24,640]{4,3,2,1,0:T(8,128)(2,1)S(1)} %fusion.7), channel_id=1, source_target_pairs={{0,1},{1,0},{2,3},{3,2},{4,5},{5,4},{6,7},{7,6},{8,9},{9,8},{10,11... | collective-permute-start | bytes 1105928 | tf_op jit(solution)/shard_map/ppermute | solution.py:366
  135.4 0.0 collective-permute-done.2
  135.4 0.1 bitcast_add_fusion.1
  135.5 9.2 %collective-permute-done.3 = bf16[3,2,2,24,640]{4,3,2,1,0:T(8,128)(2,1)S(1)} collective-permute-done((bf16[3,2,2,24,640]{4,3,2,1,0:T(8,128)(2,1)S(1)}, bf16[3,2,2,24,640]{4,3,2,1,0:T(8,128)(2,1)S(1)}, u32[]{:S(2)}, u32[]{:S(2)}) %collective-permute-start.3) | collective-permute-done | bytes 368672 | tf_op jit(solution)/shard_map/ppermute | solution.py:366
  144.7 0.1 bitcast_add_fusion
  144.8 1.1 pad_maximum_fusion
  (21 shorter events, 0.2 us)
Async XLA Ops:
  0.0 10.8 %copy-start = (bf16[3,2,2,40,640]{4,3,2,1,0:T(8,128)(2,1)S(1)}, bf16[3,2,2,40,640]{4,3,2,1,0:T(8,128)(2,1)}, u32[]{:S(2)}) copy-start(bf16[3,2,2,40,640]{4,3,2,1,0:T(8,128)(2,1)} %param.6) | copy-start | bytes 1843204
  1.0 9.8 %collective-permute-start = (bf16[3,2,2,16,640]{4,3,2,1,0:T(8,128)(2,1)S(1)}, bf16[3,2,2,16,640]{4,3,2,1,0:T(8,128)(2,1)S(1)}, u32[]{:S(2)}, u32[]{:S(2)}) collective-permute-start(bf16[3,2,2,16,640]{4,3,2,1,0:T(8,128)(2,1)S(1)} %slice.34), channel_id=1, source_target_pairs={{0,1},{1,0},{2,3},{3,2},{4,5},{5,4},{6,7},{7,6},{8,9},{9,8},{10,11... | collective-permute-start | bytes 737288 | tf_op jit(solution)/shard_map/ppermute | solution.py:314
  5.1 21.6 %collective-permute-start.1 = (bf16[3,2,2,24,640]{4,3,2,1,0:T(8,128)(2,1)S(1)}, bf16[3,2,2,24,640]{4,3,2,1,0:T(8,128)(2,1)S(1)}, u32[]{:S(2)}, u32[]{:S(2)}) collective-permute-start(bf16[3,2,2,24,640]{4,3,2,1,0:T(8,128)(2,1)S(1)} %slice.36), channel_id=1, source_target_pairs={{0,1},{1,0},{2,3},{3,2},{4,5},{5,4},{6,7},{7,6},{8,9},{9,8},{10,11... | collective-permute-start | bytes 1105928 | tf_op jit(solution)/shard_map/ppermute | solution.py:314
  6.9 4.2 %copy-start.1 = (f32[40,640]{1,0:T(8,128)}, f32[40,640]{1,0:T(8,128)S(1)}, u32[]{:S(2)}) copy-start(f32[40,640]{1,0:T(8,128)S(1)} %fusion.11) | copy-start | bytes 307204
  20.0 6.7 %slice-start = ((f32[40,640]{1,0:T(8,128)}), f32[24,640]{1,0:T(8,128)S(1)}, s32[]{:S(2)}) async-start(f32[40,640]{1,0:T(8,128)} %copy-done.1), calls=%async_computation.4 | async-start | bytes 122880 | tf_op jit(solution)/shard_map/slice | solution.py:356
  20.0 21.1 %all-to-all-start = ((bf16[16,128,128]{2,1,0:T(8,128)(2,1)}), bf16[16,128,128]{2,1,0:T(8,128)(2,1)S(1)}, u32[]{:S(2)}, u32[]{:S(2)}) async-start(bf16[16,128,128]{2,1,0:T(8,128)(2,1)} %inverse_legendre.2), calls=%async_computation | async-start | bytes 1048576 | tf_op jit(solution)/shard_map/all_to_all | solution.py:358
  39.4 6.2 %copy-start.2 = (s32[640]{0:T(1024)S(1)}, s32[640]{0:T(1024)}, u32[]{:S(2)}) copy-start(s32[640]{0:T(1024)} %param.10) | copy-start | bytes 7684
  39.4 6.3 %copy-start.3 = (f32[6]{0:T(128)S(1)}, f32[6]{0:T(128)}, u32[]{:S(2)}) copy-start(f32[6]{0:T(128)} %param.8) | copy-start | bytes 76
  39.4 6.4 %copy-start.4 = (f32[6]{0:T(128)S(1)}, f32[6]{0:T(128)}, u32[]{:S(2)}) copy-start(f32[6]{0:T(128)} %param.9) | copy-start | bytes 76
  41.1 23.2 %all-to-all-start.1 = ((bf16[16,192,128]{2,1,0:T(8,128)(2,1)}), bf16[16,192,128]{2,1,0:T(8,128)(2,1)S(1)}, u32[]{:S(2)}, u32[]{:S(2)}) async-start(bf16[16,192,128]{2,1,0:T(8,128)(2,1)} %inverse_legendre.3), calls=%async_computation.1 | async-start | bytes 1572864 | tf_op jit(solution)/shard_map/all_to_all | solution.py:358
  100.3 22.8 %all-to-all-start.3 = ((bf16[16,192,128]{2,1,0:T(8,128)(2,1)}), bf16[16,192,128]{2,1,0:T(8,128)(2,1)S(1)}, u32[]{:S(2)}, u32[]{:S(2)}) async-start(bf16[16,192,128]{2,1,0:T(8,128)(2,1)} %get-tuple-element.8), calls=%async_computation.3 | async-start | bytes 1572864 | tf_op jit(solution)/shard_map/all_to_all | solution.py:362
  112.2 23.2 %collective-permute-start.2 = (bf16[3,2,2,16,640]{4,3,2,1,0:T(8,128)(2,1)S(1)}, bf16[3,2,2,16,640]{4,3,2,1,0:T(8,128)(2,1)S(1)}, u32[]{:S(2)}, u32[]{:S(2)}) collective-permute-start(bf16[3,2,2,16,640]{4,3,2,1,0:T(8,128)(2,1)S(1)} %fusion.8), channel_id=1, source_target_pairs={{0,1},{1,0},{2,3},{3,2},{4,5},{5,4},{6,7},{7,6},{8,9},{9,8},{10,11... | collective-permute-start | bytes 737288 | tf_op jit(solution)/shard_map/ppermute | solution.py:366
  133.9 10.8 %collective-permute-start.3 = (bf16[3,2,2,24,640]{4,3,2,1,0:T(8,128)(2,1)S(1)}, bf16[3,2,2,24,640]{4,3,2,1,0:T(8,128)(2,1)S(1)}, u32[]{:S(2)}, u32[]{:S(2)}) collective-permute-start(bf16[3,2,2,24,640]{4,3,2,1,0:T(8,128)(2,1)S(1)} %fusion.7), channel_id=1, source_target_pairs={{0,1},{1,0},{2,3},{3,2},{4,5},{5,4},{6,7},{7,6},{8,9},{9,8},{10,11... | collective-permute-start | bytes 1105928 | tf_op jit(solution)/shard_map/ppermute | solution.py:366

commit v3 on v2

--- a/solution.py
+++ b/solution.py
@@ -104,19 +104,96 @@
     return jnp.where(hit, 1.0, 0.0).astype(jnp.bfloat16)
 
 
-def inverse_legendre_kernel(slots, lats, lv, nw, spec_ref, leg_ref, out_ref, cut, held):
+def whole(a):
+    return pl.BlockSpec(a.shape, lambda i, n=len(a.shape): (0,) * n)
+
+
+def greet(nw, wave, lev):
+    barrier = pltpu.get_barrier_semaphore()
+
+    @pl.loop(1, nw)
+    def _(i):
+        pl.semaphore_signal(barrier, inc=1, device_id={"wave": lax.rem(wave + i, nw)}, device_id_type=pl.DeviceIdType.MESH)
+
+    pl.semaphore_signal(barrier, inc=1, device_id={"lev": 1 - lev}, device_id_type=pl.DeviceIdType.MESH)
+    pl.semaphore_wait(barrier, nw)
+
+
+def to_wave(src, dst, slot, target, sends, recvs, i):
+    return pltpu.make_async_remote_copy(
+        src_ref=src.at[target],
+        dst_ref=dst.at[slot],
+        send_sem=sends.at[i],
+        recv_sem=recvs.at[i],
+        device_id={"wave": target},
+        device_id_type=pl.DeviceIdType.MESH,
+    )
+
+
+def to_lev(src, dst, lev, send, recv):
+    return pltpu.make_async_remote_copy(
+        src_ref=src, dst_ref=dst, send_sem=send, recv_sem=recv, device_id={"lev": 1 - lev}, device_id_type=pl.DeviceIdType.MESH
+    )
+
+
+def start_exchange(nw, wave, src, dst, sends, recvs, local):
+    @pl.loop(1, nw)
+    def _(i):
+        to_wave(src, dst, wave, lax.rem(wave + i, nw), sends, recvs, i).start()
+
+    pltpu.make_async_copy(src.at[wave], dst.at[wave], local).start()
+
+
+def wait_arrivals(nw, wave, src, dst, sends, recvs, local):
+    pltpu.make_async_copy(src.at[wave], dst.at[wave], local).wait()
+
+    @pl.loop(1, nw)
+    def _(i):
+        to_wave(src, dst, lax.rem(wave + nw - i, nw), lax.rem(wave + i, nw), sends, recvs, i).wait_recv()
+
+
+def wait_sends(nw, wave, src, dst, sends, recvs):
+    @pl.loop(1, nw)
+    def _(i):
+        to_wave(src, dst, wave, lax.rem(wave + i, nw), sends, recvs, i).wait_send()
+
+
+def inverse_legendre_kernel(groups, slots, lats, lv, nw, *refs):
+    count = len(groups)
+    owns, refs = refs[:count], refs[count:]
+    weight_ref, leg_ref, refs = refs[0], refs[1], refs[2:]
+    outs, others, sents, refs = refs[:count], refs[count : 2 * count], refs[2 * count : 3 * count], refs[3 * count :]
+    cut, held, lev_send, lev_recv, sends, recvs, local = refs
     step = pl.program_id(0)
+    wave, lev = lax.axis_index("wave"), lax.axis_index("lev")
     tiles = cut.shape[0]
-    count = 8 * lv
+    rows = 8 * lv
 
     @pl.when(step == 0)
     def _():
-        for b in range(tiles):
-            cut[b] = spec_ref[:, b * LANES : (b + 1) * LANES]
+        greet(nw, wave, lev)
+        for g in range(count):
+            to_lev(owns[g], others[g], lev, lev_send.at[g], lev_recv.at[g]).start()
+
+    for g, (start, n) in enumerate(groups):
+
+        @pl.when(step == start // UNROLL)
+        def _(g=g, start=start, n=n):
+            to_lev(owns[g], others[g], lev, lev_send.at[g], lev_recv.at[g]).wait()
+            for b in range(tiles):
+                lanes = slice(b * LANES, (b + 1) * LANES)
+                scale = weight_ref[start : start + n, lanes]
+                mine = owns[g][:, lanes].astype(jnp.float32)
+                theirs = others[g][:, lanes].astype(jnp.float32)
+                for a in range(4 * lv):
+                    x, y = mine[a * n : (a + 1) * n] * scale, theirs[a * n : (a + 1) * n] * scale
+                    for half in range(2):
+                        top = ((a // 2 * 2 + half) * 2 + a % 2) * slots + start
+                        cut[b, top : top + n, :] = jnp.where(lev == half, x, y)
 
     total = None
     for j in range(UNROLL):
-        x = jnp.concatenate([cut[b, pl.ds(step * UNROLL + j, count, stride=slots), :] for b in range(tiles)], axis=1)
+        x = jnp.concatenate([cut[b, pl.ds(step * UNROLL + j, rows, stride=slots), :] for b in range(tiles)], axis=1)
         x = jnp.concatenate([x if i == j else jnp.zeros_like(x) for i in range(UNROLL)], axis=0).astype(jnp.bfloat16)
         part = lax.dot_general(leg_ref[j], x, (((1,), (1,)), ((), ())), preferred_element_type=jnp.float32)
         total = part if total is None else total + part
@@ -125,42 +202,60 @@
     for j in range(UNROLL):
         for l in range(lv):
             for b in range(blocks):
-                r = count * j + 8 * l
+                r = rows * j + 8 * l
                 held[l * blocks + b, pl.ds(step * UNROLL + j, 8, stride=slots), :] = y[r : r + 8, b * LANES : (b + 1) * LANES]
 
+    for g, (start, n) in enumerate(groups):
+
+        @pl.when(step == (start + n) // UNROLL - 1)
+        def _(g=g, start=start, n=n):
+            packed = [
+                jnp.concatenate([held[i, r * slots + start : r * slots + start + n, :] for r in range(8)], axis=0).astype(jnp.bfloat16)
+                for i in range(lv * blocks)
+            ]
+            for d in range(nw):
+                total = jnp.zeros((8 * n, LANES), jnp.float32)
+                for b in range(lats * d // LANES, (lats * (d + 1) - 1) // LANES + 1):
+                    for l in range(lv):
+                        first = max(lats * d, LANES * b)
+                        last = min(lats * (d + 1), LANES * (b + 1))
+                        sel = placed(LANES, LANES, first - LANES * b, lats * l + first - lats * d, last - first)
+                        total += jnp.dot(packed[l * blocks + b], sel, preferred_element_type=jnp.float32)
+                sents[g][d] = total.astype(jnp.bfloat16)
+            start_exchange(nw, wave, sents[g], outs[g], sends.at[g], recvs.at[g], local.at[g])
+
     @pl.when(step == slots // UNROLL - 1)
     def _():
-        for d in range(nw):
-            total = jnp.zeros((8 * slots, LANES), jnp.float32)
-            for b in range(lats * d // LANES, (lats * (d + 1) - 1) // LANES + 1):
-                for l in range(lv):
-                    first = max(lats * d, LANES * b)
-                    last = min(lats * (d + 1), LANES * (b + 1))
-                    sel = placed(LANES, LANES, first - LANES * b, lats * l + first - lats * d, last - first)
-                    total += jnp.dot(held[l * blocks + b].astype(jnp.bfloat16), sel, preferred_element_type=jnp.float32)
-            out_ref[d] = total.astype(jnp.bfloat16)
-
-
-def inverse_legendre(spec, legendre, start, slots, lv, nw):
-    _, band, rows = legendre.shape
+        for g in range(count):
+            wait_arrivals(nw, wave, sents[g], outs[g], sends.at[g], recvs.at[g], local.at[g])
+            wait_sends(nw, wave, sents[g], outs[g], sends.at[g], recvs.at[g])
+
+
+def inverse_legendre(owns, weights, legendre, groups, lv, nw):
+    slots, band, rows = legendre.shape
     lats = band // nw
+    blocks = [jax.ShapeDtypeStruct((nw, 8 * n, LANES), jnp.bfloat16) for _, n in groups]
     return pl.pallas_call(
-        lambda *refs: inverse_legendre_kernel(slots, lats, lv, nw, *refs),
+        lambda *refs: inverse_legendre_kernel(groups, slots, lats, lv, nw, *refs),
         grid=(slots // UNROLL,),
-        in_specs=[
-            pl.BlockSpec((8 * lv * slots, rows), lambda s: (0, 0)),
-            pl.BlockSpec((UNROLL, band, rows), lambda s: (s + start // UNROLL, 0, 0)),
-        ],
-        out_specs=pl.BlockSpec((nw, 8 * slots, LANES), lambda s: (0, 0, 0)),
-        out_shape=jax.ShapeDtypeStruct((nw, 8 * slots, LANES), jnp.bfloat16),
-        scratch_shapes=[
+        in_specs=[whole(a) for a in owns] + [whole(weights), pl.BlockSpec((UNROLL, band, rows), lambda s: (s, 0, 0))],
+        out_specs=[pl.BlockSpec(memory_space=pl.ANY)] * len(groups),
+        out_shape=blocks,
+        scratch_shapes=[pltpu.VMEM(a.shape, a.dtype) for a in owns]
+        + [pltpu.VMEM(a.shape, a.dtype) for a in blocks]
+        + [
             pltpu.VMEM((rows // LANES, 8 * lv * slots, LANES), jnp.float32),
             pltpu.VMEM((lv * band // LANES, 8 * slots, LANES), jnp.float32),
+            pltpu.SemaphoreType.DMA((len(groups),)),
+            pltpu.SemaphoreType.DMA((len(groups),)),
+            pltpu.SemaphoreType.DMA((len(groups), nw)),
+            pltpu.SemaphoreType.DMA((len(groups), nw)),
+            pltpu.SemaphoreType.DMA((len(groups),)),
         ],
-        compiler_params=pltpu.CompilerParams(vmem_limit_bytes=VMEM_LIMIT),
+        compiler_params=pltpu.CompilerParams(vmem_limit_bytes=VMEM_LIMIT, collective_id=0, has_side_effects=True),
         cost_estimate=pl.CostEstimate(flops=2 * slots * band * rows * 256, bytes_accessed=2 * slots * band * rows, transcendentals=0),
         name="inverse_legendre",
-    )(spec, legendre)
+    )(*owns, weights, legendre)
 
 
 def grid_kernel(steps, factor, groups, *refs):
@@ -223,7 +318,6 @@
 def grid_space(recvs, *tables):
     steps = NLON // ROWS
     waves = tables[0].shape[1]
-    whole = lambda a: pl.BlockSpec(a.shape, lambda i, n=a.ndim: (0,) * n)
     args = (*recvs, *tables)
     return pl.pallas_call(
         lambda *refs: grid_kernel(steps, 2.0 / NLON, len(recvs), *refs),
@@ -238,64 +332,111 @@
     )(*args)
 
 
-def direct_legendre_kernel(start, slots, lats, lv, wave_ref, recv_ref, leg_ref, out_ref, held, cut):
+def direct_legendre_kernel(order, slots, lats, lv, nw, *refs):
+    count = len(order)
+    backs, leg_ref, out_ref, refs = refs[:count], refs[count], refs[count + 1], refs[count + 2 :]
+    arrived, partials, lands, refs = refs[:count], refs[count : 2 * count], refs[2 * count : 3 * count], refs[3 * count :]
+    held, cut, lev_send, lev_recv, sends, recvs, local = refs
     step = pl.program_id(0)
+    wave, lev = lax.axis_index("wave"), lax.axis_index("lev")
     blocks = leg_ref.shape[1] // LANES
+    tiles = cut.shape[0]
+    base = order[0][0]
 
     @pl.when(step == 0)
     def _():
-        for b in range(blocks):
-            total = jnp.zeros((8 * slots, lv * LANES), jnp.float32)
-            for w in range(LANES * b // lats, (LANES * (b + 1) - 1) // lats + 1):
-                first = max(lats * w, LANES * b)
-                last = min(lats * (w + 1), LANES * (b + 1))
-                sel = jnp.concatenate(
-                    [placed(LANES, LANES, lats * l + first - lats * w, first - LANES * b, last - first) for l in range(lv)], axis=1
-                )
-                total += jnp.dot(recv_ref[w], sel, preferred_element_type=jnp.float32)
-            for l in range(lv):
-                held[l * blocks + b] = total[:, l * LANES : (l + 1) * LANES]
+        greet(nw, wave, lev)
+        for g in range(count):
+            start_exchange(nw, wave, backs[g], arrived[g], sends.at[g], recvs.at[g], local.at[g])
+
+    for g, (start, n) in enumerate(order):
+
+        @pl.when(step == (start - base) % slots // UNROLL)
+        def _(g=g, start=start, n=n):
+            wait_arrivals(nw, wave, backs[g], arrived[g], sends.at[g], recvs.at[g], local.at[g])
+            for b in range(blocks):
+                total = jnp.zeros((8 * n, lv * LANES), jnp.float32)
+                for w in range(LANES * b // lats, (LANES * (b + 1) - 1) // lats + 1):
+                    first = max(lats * w, LANES * b)
+                    last = min(lats * (w + 1), LANES * (b + 1))
+                    sel = jnp.concatenate(
+                        [placed(LANES, LANES, lats * l + first - lats * w, first - LANES * b, last - first) for l in range(lv)], axis=1
+                    )
+                    total += jnp.dot(arrived[g][w], sel, preferred_element_type=jnp.float32)
+                for l in range(lv):
+                    for r in range(8):
+                        top = r * slots + start
+                        held[l * blocks + b, top : top + n, :] = total[r * n : (r + 1) * n, l * LANES : (l + 1) * LANES]
 
     for j in range(UNROLL):
-        s = step * UNROLL + j
+        s = lax.rem(step * UNROLL + base, slots) + j
         x = jnp.concatenate(
             [jnp.concatenate([held[l * blocks + b, pl.ds(s, 8, stride=slots), :] for b in range(blocks)], axis=1) for l in range(lv)], axis=0
         ).astype(jnp.bfloat16)
         y = jnp.dot(x, leg_ref[j], preferred_element_type=jnp.float32)
-        k = lax.broadcasted_iota(jnp.int32, y.shape, 1)
-        y = jnp.where(k < M - wave_ref[start + s], y, 0.0)
-        for b in range(cut.shape[0]):
+        for b in range(tiles):
             cut[b, pl.ds(s, 8 * lv, stride=slots), :] = y[:, b * LANES : (b + 1) * LANES]
 
+    def halves(b, start, n):
+        found = ([], [])
+        for a in range(4 * lv):
+            x, y = [cut[b, pl.ds(((a // 2 * 2 + half) * 2 + a % 2) * slots + start, n), :] for half in range(2)]
+            found[0].append(jnp.where(lev == 0, x, y))
+            found[1].append(jnp.where(lev == 0, y, x))
+        return found
+
+    for g, (start, n) in enumerate(order):
+
+        @pl.when(step == ((start - base) % slots + n) // UNROLL - 1)
+        def _(g=g, start=start, n=n):
+            for b in range(tiles):
+                theirs = halves(b, start, n)[1]
+                partials[g][:, b * LANES : (b + 1) * LANES] = jnp.concatenate(theirs, axis=0).astype(jnp.bfloat16)
+            to_lev(partials[g], lands[g], lev, lev_send.at[g], lev_recv.at[g]).start()
+
     @pl.when(step == slots // UNROLL - 1)
     def _():
-        for b in range(cut.shape[0]):
-            out_ref[:, b * LANES : (b + 1) * LANES] = cut[b]
-
-
-def direct_legendre(my_waves, recv, legendre, start, slots, lv):
-    _, band, rows = legendre.shape
-    nw = recv.shape[0]
+        for g, (start, n) in enumerate(order):
+            wait_sends(nw, wave, backs[g], arrived[g], sends.at[g], recvs.at[g])
+        for g, (start, n) in enumerate(order):
+            to_lev(partials[g], lands[g], lev, lev_send.at[g], lev_recv.at[g]).wait()
+            for b in range(tiles):
+                lanes = slice(b * LANES, (b + 1) * LANES)
+                mine = halves(b, start, n)[0]
+                land = lands[g][:, lanes].astype(jnp.float32)
+                for a in range(4 * lv):
+                    out_ref[a * slots + start : a * slots + start + n, lanes] = mine[a] + land[a * n : (a + 1) * n]
+
+
+def direct_legendre(backs, legendre, order, lv):
+    slots, band, rows = legendre.shape
+    nw = backs[0].shape[0]
+    lats = band // nw
+    base = order[0][0] // UNROLL
+    shares = [pltpu.VMEM((4 * lv * n, rows), jnp.bfloat16) for _, n in order]
     return pl.pallas_call(
-        lambda *refs: direct_legendre_kernel(start, slots, band // nw, lv, *refs),
-        grid_spec=pltpu.PrefetchScalarGridSpec(
-            num_scalar_prefetch=1,
-            grid=(slots // UNROLL,),
-            in_specs=[
-                pl.BlockSpec(recv.shape, lambda s, w: (0, 0, 0)),
-                pl.BlockSpec((UNROLL, band, rows), lambda s, w: (s + start // UNROLL, 0, 0)),
-            ],
-            out_specs=pl.BlockSpec((8 * lv * slots, rows), lambda s, w: (0, 0)),
-            scratch_shapes=[
-                pltpu.VMEM((lv * band // LANES, 8 * slots, LANES), jnp.float32),
-                pltpu.VMEM((rows // LANES, 8 * lv * slots, LANES), jnp.float32),
-            ],
-        ),
-        out_shape=jax.ShapeDtypeStruct((8 * lv * slots, rows), jnp.float32),
-        compiler_params=pltpu.CompilerParams(vmem_limit_bytes=VMEM_LIMIT),
+        lambda *refs: direct_legendre_kernel(order, slots, lats, lv, nw, *refs),
+        grid=(slots // UNROLL,),
+        in_specs=[pl.BlockSpec(memory_space=pl.ANY)] * len(order)
+        + [pl.BlockSpec((UNROLL, band, rows), lambda s: (lax.rem(s + base, slots // UNROLL), 0, 0))],
+        out_specs=pl.BlockSpec((4 * lv * slots, rows), lambda s: (0, 0)),
+        out_shape=jax.ShapeDtypeStruct((4 * lv * slots, rows), jnp.float32),
+        scratch_shapes=[pltpu.VMEM(a.shape, a.dtype) for a in backs]
+        + shares
+        + shares
+        + [
+            pltpu.VMEM((lv * band // LANES, 8 * slots, LANES), jnp.float32),
+            pltpu.VMEM((rows // LANES, 8 * lv * slots, LANES), jnp.float32),
+            pltpu.SemaphoreType.DMA((len(order),)),
+            pltpu.SemaphoreType.DMA((len(order),)),
+            pltpu.SemaphoreType.DMA((len(order), nw)),
+            pltpu.SemaphoreType.DMA((len(order), nw)),
+            pltpu.SemaphoreType.DMA((len(order),)),
+        ],
+        compiler_params=pltpu.CompilerParams(vmem_limit_bytes=VMEM_LIMIT, collective_id=1, has_side_effects=True),
         cost_estimate=pl.CostEstimate(flops=2 * slots * band * rows * 256, bytes_accessed=2 * slots * band * rows, transcendentals=0),
         name="direct_legendre",
-    )(my_waves, recv, legendre)
+    )(*backs, legendre)
 
 
 def body(spectral, legendre, thickness, pressure_step, wave_order, lat_order):
@@ -305,13 +446,9 @@
     slots, band, rows = legendre.shape
     lats = band // nw
     lv = spectral.shape[0]
-    swap = [(0, 1), (1, 0)]
-    upper = lev_index == 0
-
     cutoff = slots * 2 // 5 // 8 * 8
     groups = [(0, cutoff), (cutoff, slots - cutoff)] if cutoff else [(0, slots)]
-    own = [spectral[:, :, :, start : start + n] for start, n in groups]
-    others = [lax.ppermute(x, "lev", swap) for x in own]
+    owns = [spectral[:, :, :, start : start + n].reshape(4 * lv * n, rows) for start, n in groups]
     my_waves = lax.dynamic_slice(wave_order, (wave_index * slots,), (slots,))
     in_triangle = jnp.arange(rows, dtype=jnp.int32)[None, :] < (M - my_waves)[:, None]
     weights = jnp.where(my_waves == 0, 1.0, 2.0).astype(jnp.float32)[:, None]
@@ -350,21 +487,10 @@
     down = (same & (level[:, None] <= level[None, :])).astype(jnp.bfloat16)
     up = (same & (level[:, None] >= level[None, :])).astype(jnp.bfloat16)
 
-    recvs = []
-    for (start, n), x, other in zip(groups, own, others):
-        halves = jnp.stack([jnp.where(upper, x, other), jnp.where(upper, other, x)], axis=2)
-        spec = (halves.astype(jnp.float32) * weights[start : start + n]).reshape(8 * lv * n, rows)
-        sent = inverse_legendre(spec, legendre, start, n, lv, nw)
-        recvs.append(lax.all_to_all(sent, "wave", split_axis=0, concat_axis=0, tiled=True))
+    recvs = inverse_legendre(owns, weights, legendre, groups, lv, nw)
     backs = grid_space(recvs, cos_base, sin_base, row_table, lane_values, down, up)
-    results = []
-    for (start, n), back in reversed(list(zip(groups, backs))):
-        back = lax.all_to_all(back, "wave", split_axis=0, concat_axis=0, tiled=True)
-        out = direct_legendre(my_waves, back, legendre, start, n, lv).reshape(lv, 2, 2, 2, n, rows)
-        mine = jnp.where(upper, out[:, :, 0], out[:, :, 1])
-        theirs = jnp.where(upper, out[:, :, 1], out[:, :, 0]).astype(jnp.bfloat16)
-        results.append(mine + lax.ppermute(theirs, "lev", swap).astype(jnp.float32))
-    return jnp.concatenate(results[::-1], axis=3)
+    out = direct_legendre(backs[::-1], legendre, groups[::-1], lv).reshape(lv, 2, 2, slots, rows)
+    return jnp.where(in_triangle, out, 0.0)
 
 
 def solution(mesh):

time: 147 us -> 132 us (0.90)
  the two profiles are of different devices: /device:TPU:0 before, /device:TPU:13 now
where the time goes in v3:
time: 132 us
  Pallas kernels  117 us (89%)
  other arithmetic  10.5 us (8%)
  local copies, waits for them, and re-layouts  4.41 us (3%)
    pallas_call x1, Pallas kernels, direct_legendre(): pl.pallas_call(lambda *refs: direct_legendre_kernel(order, slots, lats, l...  52 us
    pallas_call x1, Pallas kernels, inverse_legendre(): pl.pallas_call(lambda *refs: inverse_legendre_kernel(groups, slots, lats,...  49.4 us
    pallas_call x1, Pallas kernels, grid_space(): pl.pallas_call(lambda *refs: grid_kernel(steps, 2.0 / NLON, len(recvs), *...  15.4 us
    select_n x1, other arithmetic, body(): jnp.where(imaginary, -sin_outer, cos_outer)  3.77 us

profile of v3, /device:TPU:13, one launch (start us, length us, event | category | flops | bytes accessed | tf_op | source)
XLA Modules:
  0.0 131.8 jit_solution(7092806146745826872)
XLA Ops:
  0.0 0.8 fusion.24
  0.8 0.1 mul.147
  0.9 0.1 mul.149
  1.0 0.7 mul.139
  1.8 0.1 mul.140
  1.8 0.1 mul.141
  1.9 0.7 mul.142
  2.7 0.1 mul.143
  2.7 0.1 mul.144
  2.9 0.8 broadcast_subtract_fusion
  3.6 0.8 compare_select_fusion
  4.4 0.1 broadcast_select_fusion.3.refs_2_
  4.5 1.0 slice.13
  5.5 1.0 slice.12
  6.5 0.0 copy-start
  6.5 49.4 %inverse_legendre.1 = (bf16[16,128,128]{2,1,0:T(8,128)(2,1)S(1)}, bf16[16,192,128]{2,1,0:T(8,128)(2,1)S(1)}) custom-call(bf16[192,640]{1,0:T(8,128)(2,1)S(1)} %bitcast.12, bf16[288,640]{1,0:T(8,128)(2,1)S(1)} %bitcast.11, f32[40,640]{1,0:T(8,128)S(1)} %broadcast_select_fusion.3.refs_2_, bf16[40,640,640]{2,1,0:T(8,128)(2,1)} %refs_2_.1), custom_call_target="tpu_custom_call" | custom-call | flops 8388608000 | bytes 32768000 | tf_op jit(solution)/shard_map/inverse_legendre/pallas_call | solution.py:238
  55.9 0.0 copy-done
  55.9 0.1 reshape.282
  56.0 0.1 slice.17
  56.1 0.1 reshape.284
  56.2 0.1 reshape.283
  56.4 3.8 %broadcast_select_fusion.2 = (f32[20,1,1280]{2,1,0:T(1,128)S(1)}, f32[20,1,1280]{2,1,0:T(1,128)S(1)}) fusion(pred[1280]{0:T(1024)(128)(4,1)S(1)} %pad_add_fusion, s32[20]{0:T(128)S(1)} %iota_multiply_fusion, s32[1280]{0:T(1024)S(1)} %add_reduce_fusion), kind=kLoop, calls=%fused_computation.16 | loop fusion | flops 307200 | bytes 211280 | tf_op jit(solution)/shard_map/jit(_where)/select_n | solution.py:467
  60.2 0.2 pad_maximum_fusion.refs_4_
  60.4 2.6 %fusion.4 = (f32[128,1280]{1,0:T(8,128)S(1)}, f32[128,1280]{1,0:T(8,128)S(1)}) fusion(s32[1280]{0:T(1024)S(1)} %add_reduce_fusion), kind=kLoop, calls=%fused_computation.6 | loop fusion | flops 1474560 | bytes 1315840 | tf_op jit(solution)/shard_map/sin | solution.py:464
  63.0 0.2 and_convert_fusion
  63.2 15.4 %grid_space.1 = (bf16[16,128,128]{2,1,0:T(8,128)(2,1)S(1)}, bf16[16,192,128]{2,1,0:T(8,128)(2,1)S(1)}) custom-call(bf16[16,128,128]{2,1,0:T(8,128)(2,1)S(1)} %get-tuple-element.9.refs_0_, bf16[16,192,128]{2,1,0:T(8,128)(2,1)S(1)} %get-tuple-element.10.refs_1_, f32[128,1280]{1,0:T(8,128)S(1)} %get-tuple-element.18.refs_2_, ...), custom_call_target="tpu_custom_call" | custom-call | flops 6710886400 | bytes 1310720 | tf_op jit(solution)/shard_map/grid_space/pallas_call | solution.py:322
  78.6 52.0 %direct_legendre.1 = f32[480,640]{1,0:T(8,128)S(1)} custom-call(bf16[16,192,128]{2,1,0:T(8,128)(2,1)S(1)} %get-tuple-element.11.refs_0_, bf16[16,128,128]{2,1,0:T(8,128)(2,1)S(1)} %get-tuple-element.12.refs_1_, bf16[40,640,640]{2,1,0:T(8,128)(2,1)} %refs_2_.1), custom_call_target="tpu_custom_call" | custom-call | flops 8388608000 | bytes 32768000 | tf_op jit(solution)/shard_map/direct_legendre/pallas_call | solution.py:417
  130.6 0.1 iota_compare_fusion
  130.7 1.1 broadcast_select_fusion
  (19 shorter events, 0.2 us)
Async XLA Ops:
  6.5 49.4 %copy-start = (s32[640]{0:T(1024)S(1)}, s32[640]{0:T(1024)}, u32[]{:S(2)}) copy-start(s32[640]{0:T(1024)} %param.10) | copy-start | bytes 7684

commit v4 on v2

v4 whole, which is shorter than its diff:
```python
import math

import jax
import jax.numpy as jnp
from jax import lax
from jax.experimental import pallas as pl
from jax.experimental.pallas import tpu as pltpu
from jax.sharding import PartitionSpec as P

M = 640
NLAT = 1280
NLON = 2560


def wave_tables(wave_list, lon_total):
    lon_ids = jnp.arange(lon_total, dtype=jnp.int32)
    phases = wave_list[:, None] * lon_ids[None, :] % lon_total
    angles = phases.astype(jnp.float32) * (2.0 * math.pi / lon_total)
    cosine = jnp.cos(angles)
    sine_part = jnp.sin(angles)
    weights = jnp.where(wave_list == 0, 1.0, 2.0).astype(jnp.float32)[:, None]
    inverse = jnp.stack([weights * cosine, -(weights * sine_part)], axis=0).astype(jnp.bfloat16)
    factor = 2.0 / lon_total
    direct = jnp.stack([factor * cosine, -(factor * sine_part)], axis=0)
    direct = jnp.transpose(direct, (2, 0, 1)).astype(jnp.bfloat16)
    return (inverse, direct)


def mix_levels(temper, diverg, geopot, omega_vel, sin_lat):
    first_field = geopot + omega_vel * temper
    second_field = sin_lat[None, :, None] * omega_vel + diverg * temper
    return jnp.stack([first_field, second_field], axis=1).astype(jnp.bfloat16)


def general_body(spectral, legendre, thickness, pressure_step, wave_order, lat_order):
    wave_index = lax.axis_index("wave")
    wave_count = lax.axis_size("wave")
    local_slots = legendre.shape[0]
    grid_lats = NLAT // wave_count
    my_waves = lax.dynamic_slice(wave_order, (wave_index * local_slots,), (local_slots,))
    row_ids = jnp.arange(M, dtype=jnp.int32)
    in_triangle = row_ids[None, :] < (M - my_waves)[:, None]
    masked_leg = jnp.where(in_triangle[:, None, :], legendre, jnp.zeros((), jnp.bfloat16))
    fourier = jnp.einsum(
        "lfcsk,sqk->lfcsq",
        lax.all_gather(spectral, "lev", axis=0, tiled=True),
        masked_leg,
        preferred_element_type=jnp.float32,
    ).astype(jnp.bfloat16)
    level_split = lax.all_to_all(fourier, "lev", split_axis=0, concat_axis=4, tiled=True)
    inverse_table, forward_legendre_table = wave_tables(wave_order, NLON)
    grid_vals = jnp.einsum(
        "lfcsq,cst->lfqt",
        lax.all_to_all(level_split, "wave", split_axis=4, concat_axis=3, tiled=True),
        inverse_table,
        preferred_element_type=jnp.float32,
    )
    lat_ids = lax.dynamic_slice(lat_order, (wave_index * grid_lats,), (grid_lats,))
    angles = math.pi * (lat_ids.astype(jnp.float32) + 0.75) / (NLAT + 0.5)
    sin_lat = jnp.cos(angles)
    cos_lat = jnp.sin(angles)
    columns = lax.all_to_all(grid_vals, "lev", split_axis=3, concat_axis=0, tiled=True)
    temper = columns[:, 0]
    diverg = columns[:, 1]
    geopot = jnp.flip(jnp.cumsum(jnp.flip(thickness[:, None, None] * temper, 0), axis=0), 0)
    omega_vel = -jnp.cumsum(pressure_step[:, None, None] * diverg, axis=0)
    tend_cols = mix_levels(temper, diverg, geopot, omega_vel, sin_lat)
    tendency_field = lax.all_to_all(tend_cols, "lev", split_axis=0, concat_axis=3, tiled=True)
    returned_grid_values = (
        jnp.einsum(
            "opgu,ukh->opkhg",
            tendency_field,
            forward_legendre_table,
            preferred_element_type=jnp.float32,
        )
        * cos_lat
    ).astype(jnp.bfloat16)
    band_vals = lax.all_to_all(
        lax.all_to_all(returned_grid_values, "wave", split_axis=3, concat_axis=4, tiled=True),
        "lev",
        split_axis=4,
        concat_axis=0,
        tiled=True,
    )
    summed = lax.psum_scatter(
        jnp.einsum("lfcsq,sqk->lfcsk", band_vals, masked_leg, preferred_element_type=jnp.float32),
        "lev",
        scatter_dimension=0,
        tiled=True,
    )
    return summed


LANES = 128
ROWS = 640
GROUP = 8
UNROLL = 4
VMEM_LIMIT = 48 * 1024 * 1024


def placed(rows, cols, row_start, col_start, count):
    r = lax.broadcasted_iota(jnp.int32, (rows, cols), 0)
    c = lax.broadcasted_iota(jnp.int32, (rows, cols), 1)
    hit = (r - row_start == c - col_start) & (c >= col_start) & (c < col_start + count)
    return jnp.where(hit, 1.0, 0.0).astype(jnp.bfloat16)


def whole(a):
    return pl.BlockSpec(a.shape, lambda i, n=len(a.shape): (0,) * n)


def greet(nw, wave, lev):
    barrier = pltpu.get_barrier_semaphore()

    @pl.loop(1, nw)
    def _(i):
        pl.semaphore_signal(barrier, inc=1, device_id={"wave": lax.rem(wave + i, nw)}, device_id_type=pl.DeviceIdType.MESH)

    pl.semaphore_signal(barrier, inc=1, device_id={"lev": 1 - lev}, device_id_type=pl.DeviceIdType.MESH)
    pl.semaphore_wait(barrier, nw)


def to_wave(src, dst, slot, target, sends, recvs, i):
    return pltpu.make_async_remote_copy(
        src_ref=src.at[target],
        dst_ref=dst.at[slot],
        send_sem=sends.at[i],
        recv_sem=recvs.at[i],
        device_id={"wave": target},
        device_id_type=pl.DeviceIdType.MESH,
    )


def to_lev(src, dst, lev, send, recv):
    return pltpu.make_async_remote_copy(
        src_ref=src, dst_ref=dst, send_sem=send, recv_sem=recv, device_id={"lev": 1 - lev}, device_id_type=pl.DeviceIdType.MESH
    )


def start_exchange(nw, wave, src, dst, sends, recvs, local):
    @pl.loop(1, nw)
    def _(i):
        to_wave(src, dst, wave, lax.rem(wave + i, nw), sends, recvs, i).start()

    pltpu.make_async_copy(src.at[wave], dst.at[wave], local).start()


def wait_arrivals(nw, wave, src, dst, sends, recvs, local):
    pltpu.make_async_copy(src.at[wave], dst.at[wave], local).wait()

    @pl.loop(1, nw)
    def _(i):
        to_wave(src, dst, lax.rem(wave + nw - i, nw), lax.rem(wave + i, nw), sends, recvs, i).wait_recv()


def wait_sends(nw, wave, src, dst, sends, recvs):
    @pl.loop(1, nw)
    def _(i):
        to_wave(src, dst, wave, lax.rem(wave + i, nw), sends, recvs, i).wait_send()


def fill_tables(waves, cos_ref, sin_ref, row_ref):
    turn = 2.0 * math.pi / NLON

    def angle(times):
        phase = waves * times
        return (phase - NLON * jnp.floor((phase + 0.5) * (1.0 / NLON))) * turn

    inner = angle(lax.broadcasted_iota(jnp.int32, cos_ref.shape, 0).astype(jnp.float32))
    cos_ref[...] = jnp.cos(inner)
    sin_ref[...] = jnp.sin(inner)
    blocks = row_ref.shape[1]
    outer = angle(lax.broadcasted_iota(jnp.int32, row_ref.shape[1:], 0).astype(jnp.float32) * float(LANES))
    cosine, sine = jnp.cos(outer), jnp.sin(outer)
    imaginary = lax.broadcasted_iota(jnp.int32, cosine.shape, 1) // GROUP % 2 == 1
    row_ref[0] = jnp.where(imaginary, -sine, cosine)
    row_ref[1] = jnp.where(imaginary, cosine, sine)


def inverse_legendre_kernel(slots, lats, lv, nw, *refs):
    wave_ref, lane_wave_ref, own, leg_ref, out, cos_ref, sin_ref, row_ref = refs[:8]
    other, sent, cut, held, lev_send, lev_recv, sends, recvs, local = refs[8:]
    step = pl.program_id(0)
    wave, lev = lax.axis_index("wave"), lax.axis_index("lev")
    tiles = cut.shape[0]
    rows = 8 * lv
    n = GROUP
    count = slots // n
    per_group = n // UNROLL

    @pl.when(step == 0)
    def _():
        greet(nw, wave, lev)
        for g in range(count):
            to_lev(own.at[g], other.at[g], lev, lev_send.at[g], lev_recv.at[g]).start()

    @pl.when(lax.rem(step, per_group) == 0)
    def _():
        g = step // per_group
        to_lev(own.at[g], other.at[g], lev, lev_send.at[g], lev_recv.at[g]).wait()
        for b in range(tiles):
            lanes = slice(b * LANES, (b + 1) * LANES)
            mine = own[g, :, lanes].astype(jnp.float32)
            theirs = other[g, :, lanes].astype(jnp.float32)
            for a in range(4 * lv):
                x, y = mine[a * n : (a + 1) * n], theirs[a * n : (a + 1) * n]
                for half in range(2):
                    top = ((a // 2 * 2 + half) * 2 + a % 2) * n
                    cut[b, top : top + n, :] = jnp.where(lev == half, x, y)

    total = None
    for j in range(UNROLL):
        s = lax.rem(step, per_group) * UNROLL + j
        m = wave_ref[wave * slots + step * UNROLL + j]
        x = jnp.concatenate([cut[b, pl.ds(s, rows, stride=n), :] for b in range(tiles)], axis=1)
        k = lax.broadcasted_iota(jnp.int32, x.shape, 1)
        x = jnp.where(k < M - m, x * jnp.where(m == 0, 1.0, 2.0), 0.0)
        x = jnp.concatenate([x if i == j else jnp.zeros_like(x) for i in range(UNROLL)], axis=0).astype(jnp.bfloat16)
        part = lax.dot_general(leg_ref[j], x, (((1,), (1,)), ((), ())), preferred_element_type=jnp.float32)
        total = part if total is None else total + part
    y = total.T
    blocks = y.shape[1] // LANES
    for j in range(UNROLL):
        s = lax.rem(step, per_group) * UNROLL + j
        for l in range(lv):
            for b in range(blocks):
                r = rows * j + 8 * l
                held[l * blocks + b, pl.ds(s, 8, stride=n), :] = y[r : r + 8, b * LANES : (b + 1) * LANES]

    @pl.when(lax.rem(step, per_group) == per_group - 1)
    def _():
        g = step // per_group
        packed = [held[i].astype(jnp.bfloat16) for i in range(lv * blocks)]
        for d in range(nw):
            total = jnp.zeros((8 * n, LANES), jnp.float32)
            for b in range(lats * d // LANES, (lats * (d + 1) - 1) // LANES + 1):
                for l in range(lv):
                    first = max(lats * d, LANES * b)
                    last = min(lats * (d + 1), LANES * (b + 1))
                    sel = placed(LANES, LANES, first - LANES * b, lats * l + first - lats * d, last - first)
                    total += jnp.dot(packed[l * blocks + b], sel, preferred_element_type=jnp.float32)
            sent[g, d] = total.astype(jnp.bfloat16)
        start_exchange(nw, wave, sent.at[g], out.at[g], sends.at[g], recvs.at[g], local.at[g])

    @pl.when(step == slots // UNROLL - 1)
    def _():
        fill_tables(lane_wave_ref[...], cos_ref, sin_ref, row_ref)

        @pl.loop(0, count)
        def _(g):
            wait_arrivals(nw, wave, sent.at[g], out.at[g], sends.at[g], recvs.at[g], local.at[g])
            wait_sends(nw, wave, sent.at[g], out.at[g], sends.at[g], recvs.at[g])


def inverse_legendre(wave_order, lane_waves, own, legendre, lv, nw):
    slots, band, rows = legendre.shape
    lats = band // nw
    count = slots // GROUP
    waves = lane_waves.shape[1]
    block = jax.ShapeDtypeStruct((count, nw, 8 * GROUP, LANES), jnp.bfloat16)
    base = jax.ShapeDtypeStruct((LANES, waves), jnp.float32)
    row = jax.ShapeDtypeStruct((2, NLON // 2 // LANES, waves), jnp.float32)
    return pl.pallas_call(
        lambda *refs: inverse_legendre_kernel(slots, lats, lv, nw, *refs),
        grid=(slots // UNROLL,),
        in_specs=[
            pl.BlockSpec(memory_space=pltpu.SMEM),
            whole(lane_waves),
            whole(own),
            pl.BlockSpec((UNROLL, band, rows), lambda s: (s, 0, 0)),
        ],
        out_specs=[pl.BlockSpec(memory_space=pl.ANY), whole(base), whole(base), whole(row)],
        out_shape=[block, base, base, row],
        scratch_shapes=[
            pltpu.VMEM(own.shape, own.dtype),
            pltpu.VMEM(block.shape, block.dtype),
            pltpu.VMEM((rows // LANES, 8 * lv * GROUP, LANES), jnp.float32),
            pltpu.VMEM((lv * band // LANES, 8 * GROUP, LANES), jnp.float32),
            pltpu.SemaphoreType.DMA((count,)),
            pltpu.SemaphoreType.DMA((count,)),
            pltpu.SemaphoreType.DMA((count, nw)),
            pltpu.SemaphoreType.DMA((count, nw)),
            pltpu.SemaphoreType.DMA((count,)),
        ],
        compiler_params=pltpu.CompilerParams(vmem_limit_bytes=VMEM_LIMIT, collective_id=0, has_side_effects=True),
        cost_estimate=pl.CostEstimate(flops=2 * slots * band * rows * 256, bytes_accessed=2 * slots * band * rows, transcendentals=0),
        name="inverse_legendre",
    )(wave_order, lane_waves, own, legendre)


def grid_kernel(steps, factor, recv, cos_ref, sin_ref, row_ref, lane_ref, sign_ref, down_ref, up_ref, out, operand, total, signs):
    i = pl.program_id(0)
    half = recv.shape[2] // 4
    waves = operand.shape[0]

    @pl.when(i == 0)
    def _():
        signs[...] = jnp.broadcast_to(sign_ref[...], (LANES, waves)).T
        for j in range(4):
            block = recv[:, :, j * half : (j + 1) * half, :].reshape(waves, LANES)
            operand[:, j * LANES : (j + 1) * LANES] = block
            operand[:, (4 + j) * LANES : (5 + j) * LANES] = (block.astype(jnp.float32) * signs[...]).astype(jnp.bfloat16)

    parts = []
    for u in range(ROWS // LANES):
        at = i * (ROWS // LANES) + u
        parts.append(cos_ref[...] * row_ref[0, pl.ds(at, 1), :] - sin_ref[...] * row_ref[1, pl.ds(at, 1), :])
    table = jnp.concatenate(parts, axis=0)

    def level_sum(x, matrix):
        high = x.astype(jnp.bfloat16)
        low = (x - high.astype(jnp.float32)).astype(jnp.bfloat16)
        return jnp.dot(high, matrix, preferred_element_type=jnp.float32) + jnp.dot(low, matrix, preferred_element_type=jnp.float32)

    values = jnp.dot(table.astype(jnp.bfloat16), operand[...], preferred_element_type=jnp.float32)
    tendency = []
    for side in range(2):
        temper = values[:, 4 * LANES * side : 4 * LANES * side + 2 * LANES]
        diverg = values[:, 4 * LANES * side + 2 * LANES : 4 * LANES * (side + 1)]
        geopot = level_sum(temper * lane_ref[0:1, :], up_ref[...])
        omega = -level_sum(diverg * lane_ref[1:2, :], down_ref[...])
        tendency.append((geopot + omega * temper).astype(jnp.bfloat16))
        tendency.append((lane_ref[2:3, :] * omega + diverg * temper).astype(jnp.bfloat16))
    tendency = jnp.concatenate(tendency, axis=1)
    part = lax.dot_general((table * factor).astype(jnp.bfloat16), tendency, (((0,), (0,)), ((), ())), preferred_element_type=jnp.float32)

    @pl.when(i == 0)
    def _():
        total[...] = part

    @pl.when(i > 0)
    def _():
        total[...] += part

    @pl.when(i == steps - 1)
    def _():
        for j in range(4):
            scale = lane_ref[3:4, j % 2 * LANES : (j % 2 + 1) * LANES]
            block = total[:, j * LANES : (j + 1) * LANES] + signs[...] * total[:, (4 + j) * LANES : (5 + j) * LANES]
            block = (block * scale).astype(jnp.bfloat16)
            out[:, :, j * half : (j + 1) * half, :] = block.reshape(recv.shape[0], recv.shape[1], half, LANES)


def grid_space(*args):
    steps = NLON // 2 // ROWS
    waves = args[1].shape[1]
    recv = args[0]
    return pl.pallas_call(
        lambda *refs: grid_kernel(steps, 2.0 / NLON, *refs),
        grid=(steps,),
        in_specs=[whole(a) for a in args],
        out_specs=whole(recv),
        out_shape=jax.ShapeDtypeStruct(recv.shape, recv.dtype),
        scratch_shapes=[
            pltpu.VMEM((waves, 8 * LANES), jnp.bfloat16),
            pltpu.VMEM((waves, 8 * LANES), jnp.float32),
            pltpu.VMEM((waves, LANES), jnp.float32),
        ],
        compiler_params=pltpu.CompilerParams(vmem_limit_bytes=VMEM_LIMIT),
        cost_estimate=pl.CostEstimate(flops=4 * NLON * waves * 4 * LANES, bytes_accessed=8 * waves * LANES, transcendentals=0),
        name="grid_space",
    )(*args)


def direct_legendre_kernel(slots, lats, lv, nw, *refs):
    wave_ref, back, leg_ref, out_ref, arrived, partial, land, held, cut, lev_send, lev_recv, sends, recvs, local = refs
    step = pl.program_id(0)
    wave, lev = lax.axis_index("wave"), lax.axis_index("lev")
    blocks = leg_ref.shape[1] // LANES
    tiles = cut.shape[0]
    n = GROUP
    count = slots // n
    per_group = n // UNROLL

    @pl.when(step == 0)
    def _():
        greet(nw, wave, lev)

        @pl.loop(0, count)
        def _(g):
            start_exchange(nw, wave, back.at[g], arrived.at[g], sends.at[g], recvs.at[g], local.at[g])

    @pl.when(lax.rem(step, per_group) == 0)
    def _():
        g = step // per_group
        wait_arrivals(nw, wave, back.at[g], arrived.at[g], sends.at[g], recvs.at[g], local.at[g])
        for b in range(blocks):
            total = jnp.zeros((8 * n, lv * LANES), jnp.float32)
            for w in range(LANES * b // lats, (LANES * (b + 1) - 1) // lats + 1):
                first = max(lats * w, LANES * b)
                last = min(lats * (w + 1), LANES * (b + 1))
                sel = jnp.concatenate(
                    [placed(LANES, LANES, lats * l + first - lats * w, first - LANES * b, last - first) for l in range(lv)], axis=1
                )
                total += jnp.dot(arrived[g, w], sel, preferred_element_type=jnp.float32)
            for l in range(lv):
                held[l * blocks + b] = total[:, l * LANES : (l + 1) * LANES]

    for j in range(UNROLL):
        s = lax.rem(step, per_group) * UNROLL + j
        x = jnp.concatenate(
            [jnp.concatenate([held[l * blocks + b, pl.ds(s, 8, stride=n), :] for b in range(blocks)], axis=1) for l in range(lv)], axis=0
        ).astype(jnp.bfloat16)
        y = jnp.dot(x, leg_ref[j], preferred_element_type=jnp.float32)
        k = lax.broadcasted_iota(jnp.int32, y.shape, 1)
        y = jnp.where(k < M - wave_ref[wave * slots + step * UNROLL + j], y, 0.0)
        for b in range(tiles):
            cut[b, pl.ds(s, 8 * lv, stride=n), :] = y[:, b * LANES : (b + 1) * LANES]

    @pl.when(lax.rem(step, per_group) == per_group - 1)
    def _():
        g = step // per_group
        start = pl.multiple_of(g * n, n)
        for b in range(tiles):
            lanes = slice(b * LANES, (b + 1) * LANES)
            theirs = []
            for a in range(4 * lv):
                x, y = [cut[b, pl.ds(((a // 2 * 2 + half) * 2 + a % 2) * n, n), :] for half in range(2)]
                theirs.append(jnp.where(lev == 0, y, x))
                out_ref[pl.ds(a * slots + start, n), lanes] = jnp.where(lev == 0, x, y)
            partial[g, :, lanes] = jnp.concatenate(theirs, axis=0).astype(jnp.bfloat16)
        to_lev(partial.at[g], land.at[g], lev, lev_send.at[g], lev_recv.at[g]).start()

    @pl.when(step == slots // UNROLL - 1)
    def _():
        @pl.loop(0, count)
        def _(g):
            wait_sends(nw, wave, back.at[g], arrived.at[g], sends.at[g], recvs.at[g])

        for g in range(count):
            to_lev(partial.at[g], land.at[g], lev, lev_send.at[g], lev_recv.at[g]).wait()
            for b in range(tiles):
                lanes = slice(b * LANES, (b + 1) * LANES)
                theirs = land[g, :, lanes].astype(jnp.float32)
                for a in range(4 * lv):
                    out_ref[a * slots + g * n : a * slots + (g + 1) * n, lanes] += theirs[a * n : (a + 1) * n]


def direct_legendre(wave_order, back, legendre, lv):
    slots, band, rows = legendre.shape
    nw = back.shape[1]
    lats = band // nw
    count = slots // GROUP
    share = pltpu.VMEM((count, 4 * lv * GROUP, rows), jnp.bfloat16)
    return pl.pallas_call(
        lambda *refs: direct_legendre_kernel(slots, lats, lv, nw, *refs),
        grid=(slots // UNROLL,),
        in_specs=[
            pl.BlockSpec(memory_space=pltpu.SMEM),
            pl.BlockSpec(memory_space=pl.ANY),
            pl.BlockSpec((UNROLL, band, rows), lambda s: (s, 0, 0)),
        ],
        out_specs=pl.BlockSpec((4 * lv * slots, rows), lambda s: (0, 0)),
        out_shape=jax.ShapeDtypeStruct((4 * lv * slots, rows), jnp.float32),
        scratch_shapes=[
            pltpu.VMEM(back.shape, back.dtype),
            share,
            share,
            pltpu.VMEM((lv * band // LANES, 8 * GROUP, LANES), jnp.float32),
            pltpu.VMEM((rows // LANES, 8 * lv * GROUP, LANES), jnp.float32),
            pltpu.SemaphoreType.DMA((count,)),
            pltpu.SemaphoreType.DMA((count,)),
            pltpu.SemaphoreType.DMA((count, nw)),
            pltpu.SemaphoreType.DMA((count, nw)),
            pltpu.SemaphoreType.DMA((count,)),
        ],
        compiler_params=pltpu.CompilerParams(vmem_limit_bytes=VMEM_LIMIT, collective_id=1, has_side_effects=True),
        cost_estimate=pl.CostEstimate(flops=2 * slots * band * rows * 256, bytes_accessed=2 * slots * band * rows, transcendentals=0),
        name="direct_legendre",
    )(wave_order, back, legendre)


def body(spectral, legendre, thickness, pressure_step, wave_order, lat_order):
    wave_index = lax.axis_index("wave")
    lev_index = lax.axis_index("lev")
    nw = lax.axis_size("wave")
    slots, band, rows = legendre.shape
    lats = band // nw
    lv = spectral.shape[0]
    count = slots // GROUP
    own = spectral.reshape(4 * lv, count, GROUP, rows).swapaxes(0, 1).reshape(count, 4 * lv * GROUP, rows)
    by_group = wave_order.reshape(nw, count, 1, GROUP).swapaxes(0, 1)
    lane_waves = jnp.broadcast_to(by_group, (count, nw, 2, GROUP)).reshape(1, -1)
    signs = (1 - 2 * (lane_waves % 2)).astype(jnp.float32)
    lane_waves = lane_waves.astype(jnp.float32)

    lat_ids = lax.dynamic_slice(lat_order, (lev_index * band + wave_index * lats,), (lats,))
    angles = math.pi * (lat_ids.astype(jnp.float32) + 0.75) / (NLAT + 0.5)

    def lanes(by_level_lat):
        pad = LANES - lv * lats
        return jnp.pad(by_level_lat.reshape(2, lv * lats), ((0, 0), (0, pad))).reshape(2 * LANES)

    spread = jnp.ones((2 * lv, lats), jnp.float32)
    zero = jnp.zeros((2 * LANES,), jnp.float32)
    lane_values = jnp.stack(
        [lanes(thickness[:, None] * spread), lanes(pressure_step[:, None] * spread), lanes(jnp.cos(angles) * spread), lanes(jnp.sin(angles) * spread)]
        + [zero] * 4
    )
    place = jnp.arange(2 * LANES)
    valid = place % LANES < lv * lats
    level = place // LANES * lv + place % LANES // lats
    lat = place % LANES % lats
    same = (lat[:, None] == lat[None, :]) & valid[:, None] & valid[None, :]
    down = (same & (level[:, None] <= level[None, :])).astype(jnp.bfloat16)
    up = (same & (level[:, None] >= level[None, :])).astype(jnp.bfloat16)

    recv, cos_base, sin_base, row_table = inverse_legendre(wave_order, lane_waves, own, legendre, lv, nw)
    back = grid_space(recv, cos_base, sin_base, row_table, lane_values, signs, down, up)
    out = direct_legendre(wave_order, back, legendre, lv)
    return out.reshape(lv, 2, 2, slots, rows)


def solution(mesh):
    nw, nl = mesh.shape["wave"], mesh.shape["lev"]

    def run(spectral, *rest):
        slots, lv = M // nw, spectral.shape[0] // nl
        fits = nl == 2 and NLAT % (nw * nl) == 0 and M % nw == 0 and slots % GROUP == 0
        fits = fits and M % LANES == 0 and lv * (NLAT // (nw * nl)) <= LANES and (NLAT // nl) % LANES == 0
        in_specs = (P("lev", None, None, "wave", None), P("wave", "lev", None), P(), P(), P(), P())
        out_specs = P("lev", None, None, "wave", None)
        chosen = body if fits else general_body
        return jax.shard_map(chosen, mesh=mesh, in_specs=in_specs, out_specs=out_specs, check_vma=False)(spectral, *rest)

    return run
```

time: 147 us -> 107 us (0.73)
  Pallas kernels: 55.9 us -> 99.9 us
  waiting for transfers between devices: 35 us -> 0 us
  starting transfers between devices: 21.3 us -> 0 us
  blocking collectives: 19.7 us -> 0 us
  other arithmetic: 10.3 us -> 1.05 us
  local copies, waits for them, and re-layouts: 3.34 us -> 5.15 us
    pallas_call x2 -> x1, Pallas kernels: 21.4 us -> 44.8 us  [inverse_legendre(): pl.pallas_call(lambda *refs: inverse_legendre_kernel(slots, lats, lv, nw,...]
    all_to_all x3 -> x0, waiting for transfers between devices: 21.9 us -> none  [the longest x2 12.4 us: body(): lax.all_to_all(sent, 'wave', split_axis=0, concat_axis=0, tiled=True)]
    pallas_call x3 -> x2, Pallas kernels: 34.6 us -> 55.2 us  [the longest x1 43.3 us: direct_legendre(): pl.pallas_call(lambda *refs: direct_legendre_kernel(slots, lats, lv, nw,...]
    all_to_all x1 -> x0, blocking collectives: 19.7 us -> none  [body(): back = lax.all_to_all(back, 'wave', split_axis=0, concat_axis=0, tiled=True)]
    all_to_all x3 -> x0, starting transfers between devices: 15.2 us -> none  [the longest x2 11.1 us: body(): lax.all_to_all(sent, 'wave', split_axis=0, concat_axis=0, tiled=True)]
    ppermute x4 -> x0, waiting for transfers between devices: 13.1 us -> none  [the longest x2 9.21 us: body(): results.append(mine + lax.ppermute(theirs, 'lev', swap).astype(jnp.float32))]
    ppermute x4 -> x0, starting transfers between devices: 6.16 us -> none  [the longest x2 3.09 us: body(): others = [lax.ppermute(x, 'lev', swap) for x in own]]
    select_n x3 -> x0, other arithmetic: 3.86 us -> none  [the longest x1 3.77 us: body(): jnp.where(imaginary, -sin_outer, cos_outer)]
  transfers between devices with their start and end apart: 7 -> 0, of which waited for: 5 -> 0; matrix products, arithmetic and copies ran while one was open for 8% -> 0% of each run, Pallas kernels for 27% -> 0%
where the time goes in v4:
time: 107 us; the launch traced here: 106 us
  Pallas kernels  99.9 us (93%)
  local copies, waits for them, and re-layouts  5.15 us (5%)
    pallas_call x1, Pallas kernels, inverse_legendre(): pl.pallas_call(lambda *refs: inverse_legendre_kernel(slots, lats, lv, nw,...  44.8 us
    pallas_call x1, Pallas kernels, direct_legendre(): pl.pallas_call(lambda *refs: direct_legendre_kernel(slots, lats, lv, nw,...  43.3 us
    pallas_call x1, Pallas kernels, grid_space(): pl.pallas_call(lambda *refs: grid_kernel(steps, 2.0 / NLON, *refs), grid=...  11.9 us

profile of v4, /device:TPU:0, one launch (start us, length us, event | category | flops | bytes accessed | tf_op | source)
XLA Modules:
  0.0 106.2 jit_solution(4397665031201208536)
XLA Ops:
  0.0 0.0 copy-start
  0.0 0.8 fusion.7
  0.8 0.7 mul.68
  1.6 0.7 mul.71
  2.3 0.1 mul.79
  2.4 0.1 mul.77
  2.5 0.1 mul.72
  2.6 0.1 mul.73
  2.7 0.1 mul.69
  2.7 0.1 mul.70
  2.9 0.8 reshape.194
  3.7 0.2 reshape.195
  3.9 0.2 and_convert_fusion
  4.1 1.1 %copy.11 = bf16[12,5,8,640]{3,2,0,1:T(8,128)(2,1)S(1)} copy(bf16[12,5,8,640]{3,2,1,0:T(8,128)(2,1)} %bitcast.16) | data formatting | bytes 1228800 | tf_op jit(solution)/shard_map/reshape | solution.py:481
  5.2 0.0 copy-done
  5.2 44.8 %inverse_legendre.1 = (bf16[5,16,64,128]{3,2,1,0:T(8,128)(2,1)S(1)}, f32[128,1280]{1,0:T(8,128)S(1)}, f32[128,1280]{1,0:T(8,128)S(1)}, f32[2,10,1280]{2,1,0:T(8,128)S(1)}) custom-call(s32[640]{0:T(1024)S(1)} %copy-done, f32[1,1280]{1,0:T(1,128)S(1)} %get-tuple-element.16.refs_1_, bf16[5,96,640]{2,1,0:T(8,128)(2,1)S(1)} %bitcast.15, bf16[40,640,640]{2,1,0:T(8,128)(2,1)} %refs_2_.1), custom_call_target="tpu_custom_call" | custom-call | flops 8388608000 | bytes 32768000 | tf_op jit(solution)/shard_map/inverse_legendre/pallas_call | solution.py:263
  50.0 11.9 %grid_space.1.refs_1_ = bf16[5,16,64,128]{3,2,1,0:T(8,128)(2,1)S(1)} custom-call(bf16[5,16,64,128]{3,2,1,0:T(8,128)(2,1)S(1)} %get-tuple-element.9.refs_0_, f32[128,1280]{1,0:T(8,128)S(1)} %get-tuple-element.10.refs_1_, f32[128,1280]{1,0:T(8,128)S(1)} %get-tuple-element.11.refs_2_, f32[2,10,1280]{2,1,0:T(8,128)S(1)} %get-tuple-element.12.refs_3_, ...), custom_call_target="tpu_custom_call" | custom-call | flops 6710886400 | bytes 1310720 | tf_op jit(solution)/shard_map/grid_space/pallas_call | solution.py:348
  61.9 43.3 %direct_legendre.1 = f32[480,640]{1,0:T(8,128)S(1)} custom-call(s32[640]{0:T(1024)S(1)} %copy-done, bf16[5,16,64,128]{3,2,1,0:T(8,128)(2,1)S(1)} %grid_space.1.refs_1_, bf16[40,640,640]{2,1,0:T(8,128)(2,1)} %refs_2_.1), custom_call_target="tpu_custom_call" | custom-call | flops 8388608000 | bytes 32768000 | tf_op jit(solution)/shard_map/direct_legendre/pallas_call | solution.py:445
  105.2 1.0 copy.13
  (15 shorter events, 0.2 us)
Async XLA Ops:
  0.0 5.2 %copy-start = (s32[640]{0:T(1024)S(1)}, s32[640]{0:T(1024)}, u32[]{:S(2)}) copy-start(s32[640]{0:T(1024)} %refs_0_.3) | copy-start | bytes 7684

commit v5 on v4

--- a/solution.py
+++ b/solution.py
@@ -94,7 +94,7 @@
 LANES = 128
 ROWS = 640
 GROUP = 8
-UNROLL = 4
+UNROLL = 8
 VMEM_LIMIT = 48 * 1024 * 1024
 
 
@@ -138,8 +138,9 @@
 
 
 def start_exchange(nw, wave, src, dst, sends, recvs, local):
-    @pl.loop(1, nw)
-    def _(i):
+    @pl.loop(0, nw - 1)
+    def _(j):
+        i = nw // 2 + (1 - 2 * lax.rem(j, 2)) * ((j + 1) // 2)
         to_wave(src, dst, wave, lax.rem(wave + i, nw), sends, recvs, i).start()
 
     pltpu.make_async_copy(src.at[wave], dst.at[wave], local).start()
@@ -177,9 +178,17 @@
     row_ref[1] = jnp.where(imaginary, cosine, sine)
 
 
+def overlaps(lats, nw):
+    return [
+        (d, b, max(lats * d, LANES * b), min(lats * (d + 1), LANES * (b + 1)))
+        for d in range(nw)
+        for b in range(lats * d // LANES, (lats * (d + 1) - 1) // LANES + 1)
+    ]
+
+
 def inverse_legendre_kernel(slots, lats, lv, nw, *refs):
     wave_ref, lane_wave_ref, own, leg_ref, out, cos_ref, sin_ref, row_ref = refs[:8]
-    other, sent, cut, held, lev_send, lev_recv, sends, recvs, local = refs[8:]
+    other, sent, cut, held, sels, lev_send, lev_recv, sends, recvs, local = refs[8:]
     step = pl.program_id(0)
     wave, lev = lax.axis_index("wave"), lax.axis_index("lev")
     tiles = cut.shape[0]
@@ -193,6 +202,11 @@
         greet(nw, wave, lev)
         for g in range(count):
             to_lev(own.at[g], other.at[g], lev, lev_send.at[g], lev_recv.at[g]).start()
+        for i, (d, b, first, last) in enumerate(overlaps(lats, nw)):
+            for l in range(lv):
+                sels[i, l * LANES : (l + 1) * LANES, :] = placed(
+                    LANES, LANES, first - LANES * b, lats * l + first - lats * d, last - first
+                )
 
     @pl.when(lax.rem(step, per_group) == 0)
     def _():
@@ -230,16 +244,13 @@
     @pl.when(lax.rem(step, per_group) == per_group - 1)
     def _():
         g = step // per_group
-        packed = [held[i].astype(jnp.bfloat16) for i in range(lv * blocks)]
+        packed = [jnp.concatenate([held[l * blocks + b] for l in range(lv)], axis=1).astype(jnp.bfloat16) for b in range(blocks)]
+        totals = [None] * nw
+        for i, (d, b, _, _) in enumerate(overlaps(lats, nw)):
+            part = jnp.dot(packed[b], sels[i], preferred_element_type=jnp.float32)
+            totals[d] = part if totals[d] is None else totals[d] + part
         for d in range(nw):
-            total = jnp.zeros((8 * n, LANES), jnp.float32)
-            for b in range(lats * d // LANES, (lats * (d + 1) - 1) // LANES + 1):
-                for l in range(lv):
-                    first = max(lats * d, LANES * b)
-                    last = min(lats * (d + 1), LANES * (b + 1))
-                    sel = placed(LANES, LANES, first - LANES * b, lats * l + first - lats * d, last - first)
-                    total += jnp.dot(packed[l * blocks + b], sel, preferred_element_type=jnp.float32)
-            sent[g, d] = total.astype(jnp.bfloat16)
+            sent[g, d] = totals[d].astype(jnp.bfloat16)
         start_exchange(nw, wave, sent.at[g], out.at[g], sends.at[g], recvs.at[g], local.at[g])
 
     @pl.when(step == slots // UNROLL - 1)
@@ -276,6 +287,7 @@
             pltpu.VMEM(block.shape, block.dtype),
             pltpu.VMEM((rows // LANES, 8 * lv * GROUP, LANES), jnp.float32),
             pltpu.VMEM((lv * band // LANES, 8 * GROUP, LANES), jnp.float32),
+            pltpu.VMEM((len(overlaps(lats, nw)), lv * LANES, LANES), jnp.bfloat16),
             pltpu.SemaphoreType.DMA((count,)),
             pltpu.SemaphoreType.DMA((count,)),
             pltpu.SemaphoreType.DMA((count, nw)),
@@ -288,13 +300,27 @@
     )(wave_order, lane_waves, own, legendre)
 
 
-def grid_kernel(steps, factor, recv, cos_ref, sin_ref, row_ref, lane_ref, sign_ref, down_ref, up_ref, out, operand, total, signs):
+def grid_kernel(steps, factor, lats, lv, *refs):
+    thick_ref, press_ref, lat_ref, recv, cos_ref, sin_ref, row_ref, sign_ref, down_ref, up_ref, out, operand, total, signs, lane_ref = refs
     i = pl.program_id(0)
     half = recv.shape[2] // 4
     waves = operand.shape[0]
 
     @pl.when(i == 0)
     def _():
+        lane = lax.broadcasted_iota(jnp.int32, (8, 2 * LANES), 1)
+        level = lane // LANES * lv + lane % LANES // lats
+        thick = press = jnp.zeros(lane.shape, jnp.float32)
+        for l in range(2 * lv):
+            thick = jnp.where(level == l, thick_ref[l], thick)
+            press = jnp.where(level == l, press_ref[l], press)
+        top = (lax.axis_index("lev") * lax.axis_size("wave") + lax.axis_index("wave")) * lats
+        lat = jnp.zeros(lane.shape, jnp.int32)
+        for q in range(lats):
+            lat = jnp.where(lane % LANES % lats == q, lat_ref[top + q], lat)
+        angle = math.pi * (lat.astype(jnp.float32) + 0.75) / (NLAT + 0.5)
+        for at, row in enumerate((thick, press, jnp.cos(angle), jnp.sin(angle))):
+            lane_ref[at : at + 1, :] = row[0:1, :]
         signs[...] = jnp.broadcast_to(sign_ref[...], (LANES, waves)).T
         for j in range(4):
             block = recv[:, :, j * half : (j + 1) * half, :].reshape(waves, LANES)
@@ -341,29 +367,30 @@
             out[:, :, j * half : (j + 1) * half, :] = block.reshape(recv.shape[0], recv.shape[1], half, LANES)
 
 
-def grid_space(*args):
+def grid_space(scalars, lats, lv, *args):
     steps = NLON // 2 // ROWS
     waves = args[1].shape[1]
     recv = args[0]
     return pl.pallas_call(
-        lambda *refs: grid_kernel(steps, 2.0 / NLON, *refs),
+        lambda *refs: grid_kernel(steps, 2.0 / NLON, lats, lv, *refs),
         grid=(steps,),
-        in_specs=[whole(a) for a in args],
+        in_specs=[pl.BlockSpec(memory_space=pltpu.SMEM)] * len(scalars) + [whole(a) for a in args],
         out_specs=whole(recv),
         out_shape=jax.ShapeDtypeStruct(recv.shape, recv.dtype),
         scratch_shapes=[
             pltpu.VMEM((waves, 8 * LANES), jnp.bfloat16),
             pltpu.VMEM((waves, 8 * LANES), jnp.float32),
             pltpu.VMEM((waves, LANES), jnp.float32),
+            pltpu.VMEM((8, 2 * LANES), jnp.float32),
         ],
         compiler_params=pltpu.CompilerParams(vmem_limit_bytes=VMEM_LIMIT),
         cost_estimate=pl.CostEstimate(flops=4 * NLON * waves * 4 * LANES, bytes_accessed=8 * waves * LANES, transcendentals=0),
         name="grid_space",
-    )(*args)
+    )(*scalars, *args)
 
 
 def direct_legendre_kernel(slots, lats, lv, nw, *refs):
-    wave_ref, back, leg_ref, out_ref, arrived, partial, land, held, cut, lev_send, lev_recv, sends, recvs, local = refs
+    wave_ref, back, leg_ref, out_ref, arrived, partial, land, held, cut, sels, lev_send, lev_recv, sends, recvs, local = refs
     step = pl.program_id(0)
     wave, lev = lax.axis_index("wave"), lax.axis_index("lev")
     blocks = leg_ref.shape[1] // LANES
@@ -380,21 +407,23 @@
         def _(g):
             start_exchange(nw, wave, back.at[g], arrived.at[g], sends.at[g], recvs.at[g], local.at[g])
 
+        for i, (d, b, first, last) in enumerate(overlaps(lats, nw)):
+            for l in range(lv):
+                sels[i, :, l * LANES : (l + 1) * LANES] = placed(
+                    LANES, LANES, lats * l + first - lats * d, first - LANES * b, last - first
+                )
+
     @pl.when(lax.rem(step, per_group) == 0)
     def _():
         g = step // per_group
         wait_arrivals(nw, wave, back.at[g], arrived.at[g], sends.at[g], recvs.at[g], local.at[g])
+        totals = [None] * blocks
+        for i, (d, b, _, _) in enumerate(overlaps(lats, nw)):
+            part = jnp.dot(arrived[g, d], sels[i], preferred_element_type=jnp.float32)
+            totals[b] = part if totals[b] is None else totals[b] + part
         for b in range(blocks):
-            total = jnp.zeros((8 * n, lv * LANES), jnp.float32)
-            for w in range(LANES * b // lats, (LANES * (b + 1) - 1) // lats + 1):
-                first = max(lats * w, LANES * b)
-                last = min(lats * (w + 1), LANES * (b + 1))
-                sel = jnp.concatenate(
-                    [placed(LANES, LANES, lats * l + first - lats * w, first - LANES * b, last - first) for l in range(lv)], axis=1
-                )
-                total += jnp.dot(arrived[g, w], sel, preferred_element_type=jnp.float32)
             for l in range(lv):
-                held[l * blocks + b] = total[:, l * LANES : (l + 1) * LANES]
+                held[l * blocks + b] = totals[b][:, l * LANES : (l + 1) * LANES]
 
     for j in range(UNROLL):
         s = lax.rem(step, per_group) * UNROLL + j
@@ -458,6 +487,7 @@
             share,
             pltpu.VMEM((lv * band // LANES, 8 * GROUP, LANES), jnp.float32),
             pltpu.VMEM((rows // LANES, 8 * lv * GROUP, LANES), jnp.float32),
+            pltpu.VMEM((len(overlaps(lats, nw)), LANES, lv * LANES), jnp.bfloat16),
             pltpu.SemaphoreType.DMA((count,)),
             pltpu.SemaphoreType.DMA((count,)),
             pltpu.SemaphoreType.DMA((count, nw)),
@@ -471,8 +501,6 @@
 
 
 def body(spectral, legendre, thickness, pressure_step, wave_order, lat_order):
-    wave_index = lax.axis_index("wave")
-    lev_index = lax.axis_index("lev")
     nw = lax.axis_size("wave")
     slots, band, rows = legendre.shape
     lats = band // nw
@@ -484,19 +512,6 @@
     signs = (1 - 2 * (lane_waves % 2)).astype(jnp.float32)
     lane_waves = lane_waves.astype(jnp.float32)
 
-    lat_ids = lax.dynamic_slice(lat_order, (lev_index * band + wave_index * lats,), (lats,))
-    angles = math.pi * (lat_ids.astype(jnp.float32) + 0.75) / (NLAT + 0.5)
-
-    def lanes(by_level_lat):
-        pad = LANES - lv * lats
-        return jnp.pad(by_level_lat.reshape(2, lv * lats), ((0, 0), (0, pad))).reshape(2 * LANES)
-
-    spread = jnp.ones((2 * lv, lats), jnp.float32)
-    zero = jnp.zeros((2 * LANES,), jnp.float32)
-    lane_values = jnp.stack(
-        [lanes(thickness[:, None] * spread), lanes(pressure_step[:, None] * spread), lanes(jnp.cos(angles) * spread), lanes(jnp.sin(angles) * spread)]
-        + [zero] * 4
-    )
     place = jnp.arange(2 * LANES)
     valid = place % LANES < lv * lats
     level = place // LANES * lv + place % LANES // lats
@@ -506,7 +521,7 @@
     up = (same & (level[:, None] >= level[None, :])).astype(jnp.bfloat16)
 
     recv, cos_base, sin_base, row_table = inverse_legendre(wave_order, lane_waves, own, legendre, lv, nw)
-    back = grid_space(recv, cos_base, sin_base, row_table, lane_values, signs, down, up)
+    back = grid_space((thickness, pressure_step, lat_order), lats, lv, recv, cos_base, sin_base, row_table, signs, down, up)
     out = direct_legendre(wave_order, back, legendre, lv)
     return out.reshape(lv, 2, 2, slots, rows)
 
@@ -516,7 +531,7 @@
 
     def run(spectral, *rest):
         slots, lv = M // nw, spectral.shape[0] // nl
-        fits = nl == 2 and NLAT % (nw * nl) == 0 and M % nw == 0 and slots % GROUP == 0
+        fits = nl == 2 and NLAT % (nw * nl) == 0 and M % nw == 0 and slots % GROUP == 0 and nw % 2 == 0
         fits = fits and M % LANES == 0 and lv * (NLAT // (nw * nl)) <= LANES and (NLAT // nl) % LANES == 0
         in_specs = (P("lev", None, None, "wave", None), P("wave", "lev", None), P(), P(), P(), P())
         out_specs = P("lev", None, None, "wave", None)

time: 107 us -> 105 us (0.981)
  Pallas kernels: 99.9 us -> 102 us
  local copies, waits for them, and re-layouts: 5.15 us -> 3.2 us
    mul x10 -> x0, local copies, waits for them, and re-layouts: 1.95 us -> none  [the longest x3 0.89 us: body(): thickness[:, None] * spread]
    pallas_call x1, Pallas kernels: 44.8 us -> 46.6 us  [inverse_legendre(): pl.pallas_call(lambda *refs: inverse_legendre_kernel(slots, lats, lv, nw,...]
    pallas_call x1, Pallas kernels: 43.3 us -> 42.1 us  [direct_legendre(): pl.pallas_call(lambda *refs: direct_legendre_kernel(slots, lats, lv, nw,...]
where the time goes in v5:
time: 105 us
  Pallas kernels  102 us (97%)
  local copies, waits for them, and re-layouts  3.2 us (3%)
    pallas_call x1, Pallas kernels, inverse_legendre(): pl.pallas_call(lambda *refs: inverse_legendre_kernel(slots, lats, lv, nw,...  46.6 us
    pallas_call x1, Pallas kernels, direct_legendre(): pl.pallas_call(lambda *refs: direct_legendre_kernel(slots, lats, lv, nw,...  42.1 us
    pallas_call x1, Pallas kernels, grid_space(): pl.pallas_call(lambda *refs: grid_kernel(steps, 2.0 / NLON, lats, lv, *re...  12.9 us

profile of v5, /device:TPU:0, one launch (start us, length us, event | category | flops | bytes accessed | tf_op | source)
XLA Modules:
  0.0 105.2 jit_solution(3790198865667886736)
XLA Ops:
  0.0 0.0 copy-start
  0.0 0.8 reshape.178
  0.9 0.2 reshape.179
  1.1 0.2 and_convert_fusion
  1.3 1.1 %copy.11 = bf16[12,5,8,640]{3,2,0,1:T(8,128)(2,1)S(1)} copy(bf16[12,5,8,640]{3,2,1,0:T(8,128)(2,1)} %bitcast.12) | data formatting | bytes 1228800 | tf_op jit(solution)/shard_map/reshape | solution.py:509
  2.4 0.0 copy-done
  2.4 0.0 copy-start.1
  2.4 0.0 copy-start.2
  2.5 0.0 copy-start.3
  2.5 46.6 %inverse_legendre.1 = (bf16[5,16,64,128]{3,2,1,0:T(8,128)(2,1)S(1)}, f32[128,1280]{1,0:T(8,128)S(1)}, f32[128,1280]{1,0:T(8,128)S(1)}, f32[2,10,1280]{2,1,0:T(8,128)S(1)}) custom-call(s32[640]{0:T(1024)S(1)} %copy-done, f32[1,1280]{1,0:T(1,128)S(1)} %get-tuple-element.14.refs_1_, bf16[5,96,640]{2,1,0:T(8,128)(2,1)S(1)} %bitcast.11, bf16[40,640,640]{2,1,0:T(8,128)(2,1)} %refs_2_.3), custom_call_target="tpu_custom_call" | custom-call | flops 8388608000 | bytes 32768000 | tf_op jit(solution)/shard_map/inverse_legendre/pallas_call | solution.py:274
  49.1 0.0 copy-done.1
  49.1 0.0 copy-done.2
  49.1 0.0 copy-done.3
  49.2 12.9 %grid_space.1.refs_1_ = bf16[5,16,64,128]{3,2,1,0:T(8,128)(2,1)S(1)} custom-call(f32[6]{0:T(128)S(1)} %copy-done.2, f32[6]{0:T(128)S(1)} %copy-done.3, s32[1280]{0:T(1024)S(1)} %copy-done.1, bf16[5,16,64,128]{3,2,1,0:T(8,128)(2,1)S(1)} %get-tuple-element.9.refs_3_, f32[128,1280]{1,0:T(8,128)S(1)} %get-tuple-element.10.refs_4_, ...), custom_call_target="tpu_custom_call" | custom-call | flops 6710886400 | bytes 1310720 | tf_op jit(solution)/shard_map/grid_space/pallas_call | solution.py:374
  62.1 42.1 %direct_legendre.1 = f32[480,640]{1,0:T(8,128)S(1)} custom-call(s32[640]{0:T(1024)S(1)} %copy-done, bf16[5,16,64,128]{3,2,1,0:T(8,128)(2,1)S(1)} %grid_space.1.refs_1_, bf16[40,640,640]{2,1,0:T(8,128)(2,1)} %refs_2_.3), custom_call_target="tpu_custom_call" | custom-call | flops 8388608000 | bytes 32768000 | tf_op jit(solution)/shard_map/direct_legendre/pallas_call | solution.py:474
  104.2 1.0 copy.13
  (5 shorter events, 0.1 us)
Async XLA Ops:
  0.0 2.4 %copy-start = (s32[640]{0:T(1024)S(1)}, s32[640]{0:T(1024)}, u32[]{:S(2)}) copy-start(s32[640]{0:T(1024)} %refs_0_.5) | copy-start | bytes 7684
  2.4 46.7 %copy-start.1 = (s32[1280]{0:T(1024)S(1)}, s32[1280]{0:T(1024)}, u32[]{:S(2)}) copy-start(s32[1280]{0:T(1024)} %refs_2_.2) | copy-start | bytes 15364
  2.4 46.7 %copy-start.2 = (f32[6]{0:T(128)S(1)}, f32[6]{0:T(128)}, u32[]{:S(2)}) copy-start(f32[6]{0:T(128)} %refs_0_.4) | copy-start | bytes 76
  2.5 46.7 %copy-start.3 = (f32[6]{0:T(128)S(1)}, f32[6]{0:T(128)}, u32[]{:S(2)}) copy-start(f32[6]{0:T(128)} %refs_1_.1) | copy-start | bytes 76

commit v6 on v5

--- a/solution.py
+++ b/solution.py
@@ -138,9 +138,8 @@
 
 
 def start_exchange(nw, wave, src, dst, sends, recvs, local):
-    @pl.loop(0, nw - 1)
-    def _(j):
-        i = nw // 2 + (1 - 2 * lax.rem(j, 2)) * ((j + 1) // 2)
+    @pl.loop(1, nw)
+    def _(i):
         to_wave(src, dst, wave, lax.rem(wave + i, nw), sends, recvs, i).start()
 
     pltpu.make_async_copy(src.at[wave], dst.at[wave], local).start()

time: 105 us -> 106 us (level)
    pallas_call x1, Pallas kernels: 42.1 us -> 43.5 us  [direct_legendre(): pl.pallas_call(lambda *refs: direct_legendre_kernel(slots, lats, lv, nw,...]
    pallas_call x1, Pallas kernels: 46.6 us -> 45.6 us  [inverse_legendre(): pl.pallas_call(lambda *refs: inverse_legendre_kernel(slots, lats, lv, nw,...]
where the time goes in v6:
time: 106 us
  Pallas kernels  102 us (96%)
  local copies, waits for them, and re-layouts  3.2 us (3%)
    pallas_call x1, Pallas kernels, inverse_legendre(): pl.pallas_call(lambda *refs: inverse_legendre_kernel(slots, lats, lv, nw,...  45.6 us
    pallas_call x1, Pallas kernels, direct_legendre(): pl.pallas_call(lambda *refs: direct_legendre_kernel(slots, lats, lv, nw,...  43.5 us
    pallas_call x1, Pallas kernels, grid_space(): pl.pallas_call(lambda *refs: grid_kernel(steps, 2.0 / NLON, lats, lv, *re...  12.9 us

profile of v6, /device:TPU:0, one launch (start us, length us, event | category | flops | bytes accessed | tf_op | source)
XLA Modules:
  0.0 105.5 jit_solution(16927568970071087413)
XLA Ops:
  0.0 0.0 copy-start
  0.0 0.8 reshape.178
  0.9 0.2 reshape.179
  1.1 0.2 and_convert_fusion
  1.3 1.1 %copy.11 = bf16[12,5,8,640]{3,2,0,1:T(8,128)(2,1)S(1)} copy(bf16[12,5,8,640]{3,2,1,0:T(8,128)(2,1)} %bitcast.12) | data formatting | bytes 1228800 | tf_op jit(solution)/shard_map/reshape | solution.py:508
  2.4 0.0 copy-done
  2.4 0.0 copy-start.1
  2.4 0.0 copy-start.2
  2.5 0.0 copy-start.3
  2.5 45.6 %inverse_legendre.1 = (bf16[5,16,64,128]{3,2,1,0:T(8,128)(2,1)S(1)}, f32[128,1280]{1,0:T(8,128)S(1)}, f32[128,1280]{1,0:T(8,128)S(1)}, f32[2,10,1280]{2,1,0:T(8,128)S(1)}) custom-call(s32[640]{0:T(1024)S(1)} %copy-done, f32[1,1280]{1,0:T(1,128)S(1)} %get-tuple-element.14.refs_1_, bf16[5,96,640]{2,1,0:T(8,128)(2,1)S(1)} %bitcast.11, bf16[40,640,640]{2,1,0:T(8,128)(2,1)} %refs_2_.3), custom_call_target="tpu_custom_call" | custom-call | flops 8388608000 | bytes 32768000 | tf_op jit(solution)/shard_map/inverse_legendre/pallas_call | solution.py:273
  48.1 0.0 copy-done.1
  48.1 0.0 copy-done.2
  48.1 0.0 copy-done.3
  48.1 12.9 %grid_space.1.refs_1_ = bf16[5,16,64,128]{3,2,1,0:T(8,128)(2,1)S(1)} custom-call(f32[6]{0:T(128)S(1)} %copy-done.2, f32[6]{0:T(128)S(1)} %copy-done.3, s32[1280]{0:T(1024)S(1)} %copy-done.1, bf16[5,16,64,128]{3,2,1,0:T(8,128)(2,1)S(1)} %get-tuple-element.9.refs_3_, f32[128,1280]{1,0:T(8,128)S(1)} %get-tuple-element.10.refs_4_, ...), custom_call_target="tpu_custom_call" | custom-call | flops 6710886400 | bytes 1310720 | tf_op jit(solution)/shard_map/grid_space/pallas_call | solution.py:373
  61.0 43.5 %direct_legendre.1 = f32[480,640]{1,0:T(8,128)S(1)} custom-call(s32[640]{0:T(1024)S(1)} %copy-done, bf16[5,16,64,128]{3,2,1,0:T(8,128)(2,1)S(1)} %grid_space.1.refs_1_, bf16[40,640,640]{2,1,0:T(8,128)(2,1)} %refs_2_.3), custom_call_target="tpu_custom_call" | custom-call | flops 8388608000 | bytes 32768000 | tf_op jit(solution)/shard_map/direct_legendre/pallas_call | solution.py:473
  104.5 1.0 copy.13
  (5 shorter events, 0.1 us)
Async XLA Ops:
  0.0 2.4 %copy-start = (s32[640]{0:T(1024)S(1)}, s32[640]{0:T(1024)}, u32[]{:S(2)}) copy-start(s32[640]{0:T(1024)} %refs_0_.5) | copy-start | bytes 7684
  2.4 45.6 %copy-start.1 = (s32[1280]{0:T(1024)S(1)}, s32[1280]{0:T(1024)}, u32[]{:S(2)}) copy-start(s32[1280]{0:T(1024)} %refs_2_.2) | copy-start | bytes 15364
  2.4 45.6 %copy-start.2 = (f32[6]{0:T(128)S(1)}, f32[6]{0:T(128)}, u32[]{:S(2)}) copy-start(f32[6]{0:T(128)} %refs_0_.4) | copy-start | bytes 76
  2.5 45.6 %copy-start.3 = (f32[6]{0:T(128)S(1)}, f32[6]{0:T(128)}, u32[]{:S(2)}) copy-start(f32[6]{0:T(128)} %refs_1_.1) | copy-start | bytes 76
